TPU v7x, 512 devices: a whole 4x8x8 slice. The times are simulated.
512 devices in a mesh: seq: 32 (over y, z_hi), chan: 16 (over x, z_lo, core).
Axes of the slice: x: 4, y: 8, z: 8 (z_hi: 4, z_lo: 2; z = z_hi * 2 + z_lo), core: 2. Of those that a mesh axis runs over, the one named last changes fastest.
Arguments:
- tokens: bfloat16 [8192, 8192], P('seq', 'chan'), may hold values from -6 to 6
- in_weight: bfloat16 [3, 8192, 2048], P(None, 'chan', 'seq'), may hold values from -0.125 to 0.125
- short_filter: float32 [3, 3, 2048], P(None, None, 'chan'), may hold values from -3 to 3
- long_filter: float32 [2048, 8192], P('chan', 'seq'), may hold values from -1 to 1
- skip_gain: float32 [2048], P('chan'), may hold values from 0.5 to 1.5
Outputs:
- gated: bfloat16 [2048, 8192], P('chan', 'seq')
All inputs are finite; a program needn't handle non-finite values.
Results may differ from a plain program's by a relative error of at most 0.04.
Values may be sent and summed in bfloat16 or wider, within the bound.
A program may use at most 64 MiB of HBM per device.

v0:
```python
import math

import jax
import jax.numpy as jnp
from jax import lax
from jax.sharding import PartitionSpec as P

HIGHEST = lax.Precision.HIGHEST
TWO_PI = 2.0 * math.pi


def from_partner(value, axis, bit):
    mask = 2**bit
    pairs = [(source, source ^ mask) for source in range(lax.axis_size(axis))]
    return lax.ppermute(value, axis, pairs)


def passed_along(value, axis, steps):
    count = lax.axis_size(axis)
    first, last = (max(0, -steps), min(count, count - steps))
    return lax.ppermute(value, axis, [(source, source + steps) for source in range(first, last)])


def phase_table(row_count, col_count, period):
    left_side = lax.broadcasted_iota(jnp.int32, (row_count, col_count), 0)
    right_side = lax.broadcasted_iota(jnp.int32, (row_count, col_count), 1)
    return TWO_PI * (left_side * right_side % period).astype(jnp.float32) / period


def rotate(real_part, imag_part, angles, direction):
    cosine = jnp.cos(angles)
    sine_part = direction * jnp.sin(angles)
    if imag_part is None:
        return (real_part * cosine, real_part * sine_part)
    return (real_part * cosine - imag_part * sine_part, real_part * sine_part + imag_part * cosine)


def transform_last(real_part, imag_part, direction):
    length_last = real_part.shape[-1]
    angles = phase_table(length_last, length_last, length_last)
    cosine = jnp.cos(angles)
    sine_part = direction * jnp.sin(angles)
    out_real = jnp.matmul(real_part, cosine, precision=HIGHEST) - jnp.matmul(
        imag_part, sine_part, precision=HIGHEST
    )
    out_imag = jnp.matmul(real_part, sine_part, precision=HIGHEST) + jnp.matmul(
        imag_part, cosine, precision=HIGHEST
    )
    return (out_real, out_imag)


def spectral_product(real_part, imag_part):
    return (
        real_part[:, 0] * real_part[:, 1] - imag_part[:, 0] * imag_part[:, 1],
        real_part[:, 0] * imag_part[:, 1] + imag_part[:, 0] * real_part[:, 1],
    )


def bit_reversed(seq_rank, sections):
    reversed_rank = jnp.zeros((), jnp.int32)
    for bit_number in range(sections):
        reversed_rank = reversed_rank + seq_rank // (1 << bit_number) % 2 * (
            1 << sections - 1 - bit_number
        )
    return reversed_rank


def forward_section(real_part, imag_part, seq_rank, bit_number):
    half_span = 1 << bit_number
    other_real, other_imag = (
        from_partner(real_part.astype(jnp.bfloat16), "seq", bit_number).astype(real_part.dtype),
        from_partner(imag_part.astype(jnp.bfloat16), "seq", bit_number).astype(imag_part.dtype),
    )
    is_upper = seq_rank // half_span % 2 == 1
    angles = TWO_PI * (seq_rank % half_span).astype(jnp.float32) / (2 * half_span)
    high_real, high_imag = rotate(other_real - real_part, other_imag - imag_part, angles, -1.0)
    return (
        jnp.where(is_upper, high_real, real_part + other_real),
        jnp.where(is_upper, high_imag, imag_part + other_imag),
    )


def inverse_section(real_part, imag_part, seq_rank, bit_number):
    half_span = 1 << bit_number
    other_real, other_imag = (
        from_partner(real_part.astype(jnp.bfloat16), "seq", bit_number).astype(real_part.dtype),
        from_partner(imag_part.astype(jnp.bfloat16), "seq", bit_number).astype(imag_part.dtype),
    )
    is_upper = seq_rank // half_span % 2 == 1
    angles = TWO_PI * (seq_rank % half_span).astype(jnp.float32) / (2 * half_span)
    mine_real, mine_imag = rotate(real_part, imag_part, angles, 1.0)
    their_real, their_imag = rotate(other_real, other_imag, angles, 1.0)
    return (
        jnp.where(is_upper, other_real - mine_real, real_part + their_real),
        jnp.where(is_upper, other_imag - mine_imag, imag_part + their_imag),
    )


def pairs_convolve(signal, transform_size):
    axis_count = lax.axis_size("seq")
    sections = axis_count.bit_length() - 1
    seq_rank = lax.axis_index("seq")
    block_width = signal.shape[-1]
    positions = seq_rank * block_width + lax.broadcasted_iota(jnp.int32, (block_width,), 0)
    angles = TWO_PI * positions.astype(jnp.float32) / transform_size
    odd_real, odd_imag = rotate(signal, None, angles, -1.0)
    top_bit = sections - 1
    half_span = 1 << top_bit
    other_even, other_real, other_imag = (
        from_partner(signal.astype(jnp.bfloat16), "seq", top_bit).astype(signal.dtype),
        from_partner(odd_real.astype(jnp.bfloat16), "seq", top_bit).astype(odd_real.dtype),
        from_partner(odd_imag.astype(jnp.bfloat16), "seq", top_bit).astype(odd_imag.dtype),
    )
    is_upper = seq_rank // half_span % 2 == 1
    twist = TWO_PI * (seq_rank % half_span).astype(jnp.float32) / (2 * half_span)
    even_high_real, even_high_imag = rotate(other_even - signal, None, twist, -1.0)
    odd_high_real, odd_high_imag = rotate(other_real - odd_real, other_imag - odd_imag, twist, -1.0)
    even_real = jnp.where(is_upper, even_high_real, signal + other_even)
    even_imag = jnp.where(is_upper, even_high_imag, jnp.zeros_like(signal))
    odd_real = jnp.where(is_upper, odd_high_real, odd_real + other_real)
    odd_imag = jnp.where(is_upper, odd_high_imag, odd_imag + other_imag)
    real_part = jnp.stack([even_real, odd_real])
    imag_part = jnp.stack([even_imag, odd_imag])
    for bit_number in range(top_bit - 1, -1, -1):
        real_part, imag_part = forward_section(real_part, imag_part, seq_rank, bit_number)
    frequency = bit_reversed(seq_rank, sections)
    inner = lax.broadcasted_iota(jnp.int32, (block_width,), 0)
    inner_angles = (
        TWO_PI * (2 * inner * frequency % transform_size).astype(jnp.float32) / transform_size
    )
    real_part, imag_part = rotate(real_part, imag_part, inner_angles, -1.0)
    real_part, imag_part = transform_last(real_part, imag_part, -1.0)
    real_part, imag_part = spectral_product(real_part, imag_part)
    real_part, imag_part = transform_last(real_part, imag_part, 1.0)
    real_part, imag_part = rotate(real_part, imag_part, inner_angles, 1.0)
    for bit_number in range(sections):
        real_part, imag_part = inverse_section(real_part, imag_part, seq_rank, bit_number)
    back_real = rotate(real_part[1], imag_part[1], angles, 1.0)[0]
    return (real_part[0] + back_real) / transform_size


def per_device(tokens, in_weight, short_filter, long_filter, skip_gain):
    partial_sums = jnp.einsum(
        "td,bdc->bct",
        tokens,
        lax.all_gather(in_weight, "seq", axis=2, tiled=True),
        preferred_element_type=jnp.float32,
    )
    summed = lax.psum_scatter(
        partial_sums.astype(jnp.bfloat16), "chan", scatter_dimension=1, tiled=True
    )
    tap_count = short_filter.shape[0]
    block_width = summed.shape[2]
    edge_rows = summed[:, :, block_width - (tap_count - 1) :]
    earlier = passed_along(edge_rows, "seq", 1)
    extended = jnp.concatenate([earlier, summed], axis=2).astype(jnp.float32)
    mixed = jnp.zeros(summed.shape, jnp.float32)
    for tap_number in range(tap_count):
        begin = tap_count - 1 - tap_number
        mixed = (
            mixed
            + short_filter[tap_number][:, :, None] * extended[:, :, begin : begin + block_width]
        )
    query = mixed[0]
    drive = mixed[1] * mixed[2]
    signal = jnp.stack([drive, long_filter])
    transform_size = 2 * lax.axis_size("seq") * block_width
    convolved = pairs_convolve(signal, transform_size)
    gated = query * (convolved + skip_gain[:, None] * drive)
    return gated.astype(jnp.bfloat16)


def solution(mesh):
    placed = (
        P("seq", "chan"),
        P(None, "chan", "seq"),
        P(None, None, "chan"),
        P("chan", "seq"),
        P("chan"),
    )
    return jax.shard_map(
        per_device, mesh=mesh, in_specs=placed, out_specs=P("chan", "seq"), check_vma=False
    )
```

profile of v0, /device:TPU:6, one launch (start us, length us, event | category | flops | bytes accessed | tf_op | source)
XLA Modules:
  0.0 454.4 jit_solution(10415099154593387866)
XLA Ops:
  7.3 129.2 %all-gather.2.cloned.1.call-done = bf16[3,512,2048]{1,2,0:T(8,128)(2,1)} async-done(((bf16[3,512,64]{1,2,0:T(8,128)(2,1)}), bf16[3,512,2048]{1,2,0:T(8,128)(2,1)}) %all-gather.2.cloned.1.call-update) | async-done | bytes 6291472 | tf_op jit(solution)/shard_map/all_gather | solution.py:146
  136.6 6.3 %convolution_convert_fusion = bf16[3,2048,256]{2,1,0:T(8,128)(2,1)} fusion(bf16[3,512,2048]{1,2,0:T(8,128)(2,1)} %all-gather.2.cloned.1.call-done, bf16[256,512]{1,0:T(8,128)(2,1)S(1)} %copy-done), kind=kOutput, calls=%fused_computation | convolution fusion | flops 1612185600 | bytes 9699328 | tf_op jit(solution)/shard_map/td,bdc->bct/dot_general | solution.py:143
  142.9 62.1 %reduce-scatter.2.cloned.1.call-done = bf16[3,128,256]{2,1,0:T(8,128)(2,1)} async-done(((bf16[3,2048,256]{2,1,0:T(8,128)(2,1)}), bf16[3,128,256]{2,1,0:T(8,128)(2,1)}) %reduce-scatter.2.cloned.1.call-update) | async-done | bytes 196624 | tf_op jit(solution)/shard_map/reduce_scatter | solution.py:149
  214.6 10.8 %collective-permute-start.1 = (bf16[2,128,256]{2,1,0:T(8,128)(2,1)S(1)}, bf16[2,128,256]{2,1,0:T(8,128)(2,1)S(1)}, u32[]{:S(2)}, u32[]{:S(2)}) collective-permute-start(bf16[2,128,256]{2,1,0:T(8,128)(2,1)S(1)} %fusion.132), channel_id=1, source_target_pairs={{0,256},{16,272},{32,288},{48,304},{64,320},{80,336},{96,352},{112... | collective-permute-start | bytes 393224 | tf_op jit(solution)/shard_map/ppermute | solution.py:15
  225.7 5.2 %collective-permute-done.1 = bf16[2,128,256]{2,1,0:T(8,128)(2,1)S(1)} collective-permute-done((bf16[2,128,256]{2,1,0:T(8,128)(2,1)S(1)}, bf16[2,128,256]{2,1,0:T(8,128)(2,1)S(1)}, u32[]{:S(2)}, u32[]{:S(2)}) %collective-permute-start.1) | collective-permute-done | bytes 131104 | tf_op jit(solution)/shard_map/ppermute | solution.py:15
  231.0 8.4 %collective-permute-start.2 = (bf16[2,128,256]{2,1,0:T(8,128)(2,1)S(1)}, bf16[2,128,256]{2,1,0:T(8,128)(2,1)S(1)}, u32[]{:S(2)}, u32[]{:S(2)}) collective-permute-start(bf16[2,128,256]{2,1,0:T(8,128)(2,1)S(1)} %get-tuple-element.61), channel_id=1, source_target_pairs={{0,256},{16,272},{32,288},{48,304},{64,320},{80,336},{96,352},{112... | collective-permute-start | bytes 393224 | tf_op jit(solution)/shard_map/ppermute | solution.py:15
  241.4 5.0 %collective-permute-done.2 = bf16[2,128,256]{2,1,0:T(8,128)(2,1)S(1)} collective-permute-done((bf16[2,128,256]{2,1,0:T(8,128)(2,1)S(1)}, bf16[2,128,256]{2,1,0:T(8,128)(2,1)S(1)}, u32[]{:S(2)}, u32[]{:S(2)}) %collective-permute-start.2) | collective-permute-done | bytes 131104 | tf_op jit(solution)/shard_map/ppermute | solution.py:15
  246.4 4.8 %collective-permute-done.3 = bf16[2,128,256]{2,1,0:T(8,128)(2,1)S(1)} collective-permute-done((bf16[2,128,256]{2,1,0:T(8,128)(2,1)S(1)}, bf16[2,128,256]{2,1,0:T(8,128)(2,1)S(1)}, u32[]{:S(2)}, u32[]{:S(2)}) %collective-permute-start.3) | collective-permute-done | bytes 131104 | tf_op jit(solution)/shard_map/ppermute | solution.py:15
  253.4 4.8 %collective-permute-start.5 = (bf16[2,2,128,256]{3,2,1,0:T(8,128)(2,1)S(1)}, bf16[2,2,128,256]{3,2,1,0:T(8,128)(2,1)S(1)}, u32[]{:S(2)}, u32[]{:S(2)}) collective-permute-start(bf16[2,2,128,256]{3,2,1,0:T(8,128)(2,1)S(1)} %fusion.10), channel_id=1, source_target_pairs={{0,128},{16,144},{32,160},{48,176},{64,192},{80,208},{96,224},{112... | collective-permute-start | bytes 786440 | tf_op jit(solution)/shard_map/ppermute | solution.py:15
  258.4 14.1 %collective-permute-done.4 = bf16[2,2,128,256]{3,2,1,0:T(8,128)(2,1)S(1)} collective-permute-done((bf16[2,2,128,256]{3,2,1,0:T(8,128)(2,1)S(1)}, bf16[2,2,128,256]{3,2,1,0:T(8,128)(2,1)S(1)}, u32[]{:S(2)}, u32[]{:S(2)}) %collective-permute-start.4) | collective-permute-done | bytes 262176 | tf_op jit(solution)/shard_map/ppermute | solution.py:15
  272.5 5.5 %collective-permute-done.5 = bf16[2,2,128,256]{3,2,1,0:T(8,128)(2,1)S(1)} collective-permute-done((bf16[2,2,128,256]{3,2,1,0:T(8,128)(2,1)S(1)}, bf16[2,2,128,256]{3,2,1,0:T(8,128)(2,1)S(1)}, u32[]{:S(2)}, u32[]{:S(2)}) %collective-permute-start.5) | collective-permute-done | bytes 262176 | tf_op jit(solution)/shard_map/ppermute | solution.py:15
  285.0 5.2 %collective-permute-done.6 = bf16[2,2,128,256]{3,2,1,0:T(8,128)(2,1)S(1)} collective-permute-done((bf16[2,2,128,256]{3,2,1,0:T(8,128)(2,1)}, bf16[2,2,128,256]{3,2,1,0:T(8,128)(2,1)S(1)}, u32[]{:S(2)}, u32[]{:S(2)}) %collective-permute-start.6) | collective-permute-done | bytes 262176 | tf_op jit(solution)/shard_map/ppermute | solution.py:15
  296.9 6.7 %collective-permute-start.8 = (bf16[2,2,128,256]{3,2,1,0:T(8,128)(2,1)S(1)}, bf16[2,2,128,256]{3,2,1,0:T(8,128)(2,1)S(1)}, u32[]{:S(2)}, u32[]{:S(2)}) collective-permute-start(bf16[2,2,128,256]{3,2,1,0:T(8,128)(2,1)S(1)} %get-tuple-element.29), channel_id=1, source_target_pairs={{0,32},{16,48},{32,0},{48,16},{64,96},{80,112},{96,64},{112,80},{1... | collective-permute-start | bytes 786440 | tf_op jit(solution)/shard_map/ppermute | solution.py:15
  306.8 15.1 %collective-permute-done.8 = bf16[2,2,128,256]{3,2,1,0:T(8,128)(2,1)S(1)} collective-permute-done((bf16[2,2,128,256]{3,2,1,0:T(8,128)(2,1)S(1)}, bf16[2,2,128,256]{3,2,1,0:T(8,128)(2,1)S(1)}, u32[]{:S(2)}, u32[]{:S(2)}) %collective-permute-start.8) | collective-permute-done | bytes 262176 | tf_op jit(solution)/shard_map/ppermute | solution.py:15
  321.9 5.2 %collective-permute-done.9 = bf16[2,2,128,256]{3,2,1,0:T(8,128)(2,1)S(1)} collective-permute-done((bf16[2,2,128,256]{3,2,1,0:T(8,128)(2,1)S(1)}, bf16[2,2,128,256]{3,2,1,0:T(8,128)(2,1)S(1)}, u32[]{:S(2)}, u32[]{:S(2)}) %collective-permute-start.9) | collective-permute-done | bytes 262176 | tf_op jit(solution)/shard_map/ppermute | solution.py:15
  329.9 5.0 %collective-permute-start.11 = (bf16[2,2,128,256]{3,2,1,0:T(8,128)(2,1)S(1)}, bf16[2,2,128,256]{3,2,1,0:T(8,128)(2,1)S(1)}, u32[]{:S(2)}, u32[]{:S(2)}) collective-permute-start(bf16[2,2,128,256]{3,2,1,0:T(8,128)(2,1)S(1)} %get-tuple-element.39), channel_id=1, source_target_pairs={{0,16},{16,0},{32,48},{48,32},{64,80},{80,64},{96,112},{112,96},{1... | collective-permute-start | bytes 786440 | tf_op jit(solution)/shard_map/ppermute | solution.py:15
  335.1 16.2 %collective-permute-done.10 = bf16[2,2,128,256]{3,2,1,0:T(8,128)(2,1)S(1)} collective-permute-done((bf16[2,2,128,256]{3,2,1,0:T(8,128)(2,1)}, bf16[2,2,128,256]{3,2,1,0:T(8,128)(2,1)S(1)}, u32[]{:S(2)}, u32[]{:S(2)}) %collective-permute-start.10) | collective-permute-done | bytes 262176 | tf_op jit(solution)/shard_map/ppermute | solution.py:15
  368.6 4.8 %collective-permute-start.13 = (bf16[2,128,256]{2,1,0:T(8,128)(2,1)S(1)}, bf16[2,128,256]{2,1,0:T(8,128)(2,1)S(1)}, u32[]{:S(2)}, u32[]{:S(2)}) collective-permute-start(bf16[2,128,256]{2,1,0:T(8,128)(2,1)S(1)} %get-tuple-element.21), channel_id=1, source_target_pairs={{0,16},{16,0},{32,48},{48,32},{64,80},{80,64},{96,112},{112,96},{1... | collective-permute-start | bytes 393224 | tf_op jit(solution)/shard_map/ppermute | solution.py:15
  373.4 5.8 %collective-permute-done.12 = bf16[2,128,256]{2,1,0:T(8,128)(2,1)S(1)} collective-permute-done((bf16[2,128,256]{2,1,0:T(8,128)(2,1)S(1)}, bf16[2,128,256]{2,1,0:T(8,128)(2,1)S(1)}, u32[]{:S(2)}, u32[]{:S(2)}) %collective-permute-start.12) | collective-permute-done | bytes 131104 | tf_op jit(solution)/shard_map/ppermute | solution.py:15
  380.9 7.8 %collective-permute-start.14 = (bf16[2,128,256]{2,1,0:T(8,128)(2,1)S(1)}, bf16[2,128,256]{2,1,0:T(8,128)(2,1)S(1)}, u32[]{:S(2)}, u32[]{:S(2)}) collective-permute-start(bf16[2,128,256]{2,1,0:T(8,128)(2,1)S(1)} %get-tuple-element.53), channel_id=1, source_target_pairs={{0,32},{16,48},{32,0},{48,16},{64,96},{80,112},{96,64},{112,80},{1... | collective-permute-start | bytes 393224 | tf_op jit(solution)/shard_map/ppermute | solution.py:15
  394.6 7.4 %collective-permute-done.15 = bf16[2,128,256]{2,1,0:T(8,128)(2,1)S(1)} collective-permute-done((bf16[2,128,256]{2,1,0:T(8,128)(2,1)S(1)}, bf16[2,128,256]{2,1,0:T(8,128)(2,1)S(1)}, u32[]{:S(2)}, u32[]{:S(2)}) %collective-permute-start.15) | collective-permute-done | bytes 131104 | tf_op jit(solution)/shard_map/ppermute | solution.py:15
  419.2 5.6 %collective-permute-done.18 = bf16[2,128,256]{2,1,0:T(8,128)(2,1)S(1)} collective-permute-done((bf16[2,128,256]{2,1,0:T(8,128)(2,1)S(1)}, bf16[2,128,256]{2,1,0:T(8,128)(2,1)S(1)}, u32[]{:S(2)}, u32[]{:S(2)}) %collective-permute-start.18) | collective-permute-done | bytes 131104 | tf_op jit(solution)/shard_map/ppermute | solution.py:15
  426.3 8.4 %collective-permute-start.20 = (bf16[2,128,256]{2,1,0:T(8,128)(2,1)S(1)}, bf16[2,128,256]{2,1,0:T(8,128)(2,1)S(1)}, u32[]{:S(2)}, u32[]{:S(2)}) collective-permute-start(bf16[2,128,256]{2,1,0:T(8,128)(2,1)S(1)} %get-tuple-element.47), channel_id=1, source_target_pairs={{0,256},{16,272},{32,288},{48,304},{64,320},{80,336},{96,352},{112... | collective-permute-start | bytes 393224 | tf_op jit(solution)/shard_map/ppermute | solution.py:15
  440.0 6.7 %collective-permute-done.21 = bf16[2,128,256]{2,1,0:T(8,128)(2,1)S(1)} collective-permute-done((bf16[2,128,256]{2,1,0:T(8,128)(2,1)S(1)}, bf16[2,128,256]{2,1,0:T(8,128)(2,1)S(1)}, u32[]{:S(2)}, u32[]{:S(2)}) %collective-permute-start.21) | collective-permute-done | bytes 131104 | tf_op jit(solution)/shard_map/ppermute | solution.py:15
  (73 shorter events, 83.6 us)
Async XLA Ops:
  6.5 130.0 %all-gather.2.cloned.1.call-start = ((), (), s32[]{:S(2)}) async-start(), calls=%async_computation.1 | async-start | bytes 6488064 | tf_op jit(solution)/shard_map/all_gather | solution.py:146
  7.3 197.7 %reduce-scatter.2.cloned.1.call-start = ((), (), s32[]{:S(2)}) async-start(), calls=%async_computation.2 | async-start | bytes 3342336 | tf_op jit(solution)/shard_map/reduce_scatter | solution.py:149
  205.9 7.1 %collective-permute-start = (bf16[3,128,2]{2,1,0:T(8,128)(2,1)S(1)}, bf16[3,128,2]{2,1,0:T(8,128)(2,1)S(1)}, u32[]{:S(2)}, u32[]{:S(2)}) collective-permute-start(bf16[3,128,2]{2,1,0:T(8,128)(2,1)S(1)} %slice.72), channel_id=1, source_target_pairs={{0,16},{16,32},{32,48},{48,64},{64,80},{80,96},{96,112},{112,128},... | collective-permute-start | bytes 4616 | tf_op jit(solution)/shard_map/ppermute | solution.py:21
  214.6 16.3 %collective-permute-start.1 = (bf16[2,128,256]{2,1,0:T(8,128)(2,1)S(1)}, bf16[2,128,256]{2,1,0:T(8,128)(2,1)S(1)}, u32[]{:S(2)}, u32[]{:S(2)}) collective-permute-start(bf16[2,128,256]{2,1,0:T(8,128)(2,1)S(1)} %fusion.132), channel_id=1, source_target_pairs={{0,256},{16,272},{32,288},{48,304},{64,320},{80,336},{96,352},{112... | collective-permute-start | bytes 393224 | tf_op jit(solution)/shard_map/ppermute | solution.py:15
  231.0 15.4 %collective-permute-start.2 = (bf16[2,128,256]{2,1,0:T(8,128)(2,1)S(1)}, bf16[2,128,256]{2,1,0:T(8,128)(2,1)S(1)}, u32[]{:S(2)}, u32[]{:S(2)}) collective-permute-start(bf16[2,128,256]{2,1,0:T(8,128)(2,1)S(1)} %get-tuple-element.61), channel_id=1, source_target_pairs={{0,256},{16,272},{32,288},{48,304},{64,320},{80,336},{96,352},{112... | collective-permute-start | bytes 393224 | tf_op jit(solution)/shard_map/ppermute | solution.py:15
  239.4 11.8 %collective-permute-start.3 = (bf16[2,128,256]{2,1,0:T(8,128)(2,1)S(1)}, bf16[2,128,256]{2,1,0:T(8,128)(2,1)S(1)}, u32[]{:S(2)}, u32[]{:S(2)}) collective-permute-start(bf16[2,128,256]{2,1,0:T(8,128)(2,1)S(1)} %get-tuple-element.62), channel_id=1, source_target_pairs={{0,256},{16,272},{32,288},{48,304},{64,320},{80,336},{96,352},{112... | collective-permute-start | bytes 393224 | tf_op jit(solution)/shard_map/ppermute | solution.py:15
  251.4 21.1 %collective-permute-start.4 = (bf16[2,2,128,256]{3,2,1,0:T(8,128)(2,1)S(1)}, bf16[2,2,128,256]{3,2,1,0:T(8,128)(2,1)S(1)}, u32[]{:S(2)}, u32[]{:S(2)}) collective-permute-start(bf16[2,2,128,256]{3,2,1,0:T(8,128)(2,1)S(1)} %fusion.11), channel_id=1, source_target_pairs={{0,128},{16,144},{32,160},{48,176},{64,192},{80,208},{96,224},{112... | collective-permute-start | bytes 786440 | tf_op jit(solution)/shard_map/ppermute | solution.py:15
  253.4 24.6 %collective-permute-start.5 = (bf16[2,2,128,256]{3,2,1,0:T(8,128)(2,1)S(1)}, bf16[2,2,128,256]{3,2,1,0:T(8,128)(2,1)S(1)}, u32[]{:S(2)}, u32[]{:S(2)}) collective-permute-start(bf16[2,2,128,256]{3,2,1,0:T(8,128)(2,1)S(1)} %fusion.10), channel_id=1, source_target_pairs={{0,128},{16,144},{32,160},{48,176},{64,192},{80,208},{96,224},{112... | collective-permute-start | bytes 786440 | tf_op jit(solution)/shard_map/ppermute | solution.py:15
  279.0 11.3 %collective-permute-start.6 = (bf16[2,2,128,256]{3,2,1,0:T(8,128)(2,1)}, bf16[2,2,128,256]{3,2,1,0:T(8,128)(2,1)S(1)}, u32[]{:S(2)}, u32[]{:S(2)}) collective-permute-start(bf16[2,2,128,256]{3,2,1,0:T(8,128)(2,1)} %get-tuple-element.33), channel_id=1, source_target_pairs={{0,64},{16,80},{32,96},{48,112},{64,0},{80,16},{96,32},{112,48},{1... | collective-permute-start | bytes 786440 | tf_op jit(solution)/shard_map/ppermute | solution.py:15
  280.9 14.0 %collective-permute-start.7 = (bf16[2,2,128,256]{3,2,1,0:T(8,128)(2,1)S(1)}, bf16[2,2,128,256]{3,2,1,0:T(8,128)(2,1)S(1)}, u32[]{:S(2)}, u32[]{:S(2)}) collective-permute-start(bf16[2,2,128,256]{3,2,1,0:T(8,128)(2,1)S(1)} %get-tuple-element.43), channel_id=1, source_target_pairs={{0,64},{16,80},{32,96},{48,112},{64,0},{80,16},{96,32},{112,48},{1... | collective-permute-start | bytes 786440 | tf_op jit(solution)/shard_map/ppermute | solution.py:15
  296.9 25.1 %collective-permute-start.8 = (bf16[2,2,128,256]{3,2,1,0:T(8,128)(2,1)S(1)}, bf16[2,2,128,256]{3,2,1,0:T(8,128)(2,1)S(1)}, u32[]{:S(2)}, u32[]{:S(2)}) collective-permute-start(bf16[2,2,128,256]{3,2,1,0:T(8,128)(2,1)S(1)} %get-tuple-element.29), channel_id=1, source_target_pairs={{0,32},{16,48},{32,0},{48,16},{64,96},{80,112},{96,64},{112,80},{1... | collective-permute-start | bytes 786440 | tf_op jit(solution)/shard_map/ppermute | solution.py:15
  303.6 23.5 %collective-permute-start.9 = (bf16[2,2,128,256]{3,2,1,0:T(8,128)(2,1)S(1)}, bf16[2,2,128,256]{3,2,1,0:T(8,128)(2,1)S(1)}, u32[]{:S(2)}, u32[]{:S(2)}) collective-permute-start(bf16[2,2,128,256]{3,2,1,0:T(8,128)(2,1)S(1)} %get-tuple-element.41), channel_id=1, source_target_pairs={{0,32},{16,48},{32,0},{48,16},{64,96},{80,112},{96,64},{112,80},{1... | collective-permute-start | bytes 786440 | tf_op jit(solution)/shard_map/ppermute | solution.py:15
  328.0 23.3 %collective-permute-start.10 = (bf16[2,2,128,256]{3,2,1,0:T(8,128)(2,1)}, bf16[2,2,128,256]{3,2,1,0:T(8,128)(2,1)S(1)}, u32[]{:S(2)}, u32[]{:S(2)}) collective-permute-start(bf16[2,2,128,256]{3,2,1,0:T(8,128)(2,1)} %get-tuple-element.25), channel_id=1, source_target_pairs={{0,16},{16,0},{32,48},{48,32},{64,80},{80,64},{96,112},{112,96},{1... | collective-permute-start | bytes 786440 | tf_op jit(solution)/shard_map/ppermute | solution.py:15
  329.9 24.3 %collective-permute-start.11 = (bf16[2,2,128,256]{3,2,1,0:T(8,128)(2,1)S(1)}, bf16[2,2,128,256]{3,2,1,0:T(8,128)(2,1)S(1)}, u32[]{:S(2)}, u32[]{:S(2)}) collective-permute-start(bf16[2,2,128,256]{3,2,1,0:T(8,128)(2,1)S(1)} %get-tuple-element.39), channel_id=1, source_target_pairs={{0,16},{16,0},{32,48},{48,32},{64,80},{80,64},{96,112},{112,96},{1... | collective-permute-start | bytes 786440 | tf_op jit(solution)/shard_map/ppermute | solution.py:15
  366.7 12.6 %collective-permute-start.12 = (bf16[2,128,256]{2,1,0:T(8,128)(2,1)S(1)}, bf16[2,128,256]{2,1,0:T(8,128)(2,1)S(1)}, u32[]{:S(2)}, u32[]{:S(2)}) collective-permute-start(bf16[2,128,256]{2,1,0:T(8,128)(2,1)S(1)} %get-tuple-element.55), channel_id=1, source_target_pairs={{0,16},{16,0},{32,48},{48,32},{64,80},{80,64},{96,112},{112,96},{1... | collective-permute-start | bytes 393224 | tf_op jit(solution)/shard_map/ppermute | solution.py:15
  368.6 12.2 %collective-permute-start.13 = (bf16[2,128,256]{2,1,0:T(8,128)(2,1)S(1)}, bf16[2,128,256]{2,1,0:T(8,128)(2,1)S(1)}, u32[]{:S(2)}, u32[]{:S(2)}) collective-permute-start(bf16[2,128,256]{2,1,0:T(8,128)(2,1)S(1)} %get-tuple-element.21), channel_id=1, source_target_pairs={{0,16},{16,0},{32,48},{48,32},{64,80},{80,64},{96,112},{112,96},{1... | collective-permute-start | bytes 393224 | tf_op jit(solution)/shard_map/ppermute | solution.py:15
  380.9 13.7 %collective-permute-start.14 = (bf16[2,128,256]{2,1,0:T(8,128)(2,1)S(1)}, bf16[2,128,256]{2,1,0:T(8,128)(2,1)S(1)}, u32[]{:S(2)}, u32[]{:S(2)}) collective-permute-start(bf16[2,128,256]{2,1,0:T(8,128)(2,1)S(1)} %get-tuple-element.53), channel_id=1, source_target_pairs={{0,32},{16,48},{32,0},{48,16},{64,96},{80,112},{96,64},{112,80},{1... | collective-permute-start | bytes 393224 | tf_op jit(solution)/shard_map/ppermute | solution.py:15
  388.7 13.3 %collective-permute-start.15 = (bf16[2,128,256]{2,1,0:T(8,128)(2,1)S(1)}, bf16[2,128,256]{2,1,0:T(8,128)(2,1)S(1)}, u32[]{:S(2)}, u32[]{:S(2)}) collective-permute-start(bf16[2,128,256]{2,1,0:T(8,128)(2,1)S(1)} %get-tuple-element.17), channel_id=1, source_target_pairs={{0,32},{16,48},{32,0},{48,16},{64,96},{80,112},{96,64},{112,80},{1... | collective-permute-start | bytes 393224 | tf_op jit(solution)/shard_map/ppermute | solution.py:15
  402.2 6.9 %collective-permute-start.16 = (bf16[2,128,256]{2,1,0:T(8,128)(2,1)S(1)}, bf16[2,128,256]{2,1,0:T(8,128)(2,1)S(1)}, u32[]{:S(2)}, u32[]{:S(2)}) collective-permute-start(bf16[2,128,256]{2,1,0:T(8,128)(2,1)S(1)} %get-tuple-element.51), channel_id=1, source_target_pairs={{0,64},{16,80},{32,96},{48,112},{64,0},{80,16},{96,32},{112,48},{1... | collective-permute-start | bytes 393224 | tf_op jit(solution)/shard_map/ppermute | solution.py:15
  405.4 6.9 %collective-permute-start.17 = (bf16[2,128,256]{2,1,0:T(8,128)(2,1)S(1)}, bf16[2,128,256]{2,1,0:T(8,128)(2,1)S(1)}, u32[]{:S(2)}, u32[]{:S(2)}) collective-permute-start(bf16[2,128,256]{2,1,0:T(8,128)(2,1)S(1)} %get-tuple-element.13), channel_id=1, source_target_pairs={{0,64},{16,80},{32,96},{48,112},{64,0},{80,16},{96,32},{112,48},{1... | collective-permute-start | bytes 393224 | tf_op jit(solution)/shard_map/ppermute | solution.py:15
  412.4 12.3 %collective-permute-start.18 = (bf16[2,128,256]{2,1,0:T(8,128)(2,1)S(1)}, bf16[2,128,256]{2,1,0:T(8,128)(2,1)S(1)}, u32[]{:S(2)}, u32[]{:S(2)}) collective-permute-start(bf16[2,128,256]{2,1,0:T(8,128)(2,1)S(1)} %get-tuple-element.49), channel_id=1, source_target_pairs={{0,128},{16,144},{32,160},{48,176},{64,192},{80,208},{96,224},{112... | collective-permute-start | bytes 393224 | tf_op jit(solution)/shard_map/ppermute | solution.py:15
  414.3 11.8 %collective-permute-start.19 = (bf16[2,128,256]{2,1,0:T(8,128)(2,1)S(1)}, bf16[2,128,256]{2,1,0:T(8,128)(2,1)S(1)}, u32[]{:S(2)}, u32[]{:S(2)}) collective-permute-start(bf16[2,128,256]{2,1,0:T(8,128)(2,1)S(1)} %get-tuple-element.9), channel_id=1, source_target_pairs={{0,128},{16,144},{32,160},{48,176},{64,192},{80,208},{96,224},{112... | collective-permute-start | bytes 393224 | tf_op jit(solution)/shard_map/ppermute | solution.py:15
  426.3 13.7 %collective-permute-start.20 = (bf16[2,128,256]{2,1,0:T(8,128)(2,1)S(1)}, bf16[2,128,256]{2,1,0:T(8,128)(2,1)S(1)}, u32[]{:S(2)}, u32[]{:S(2)}) collective-permute-start(bf16[2,128,256]{2,1,0:T(8,128)(2,1)S(1)} %get-tuple-element.47), channel_id=1, source_target_pairs={{0,256},{16,272},{32,288},{48,304},{64,320},{80,336},{96,352},{112... | collective-permute-start | bytes 393224 | tf_op jit(solution)/shard_map/ppermute | solution.py:15
  434.7 12.0 %collective-permute-start.21 = (bf16[2,128,256]{2,1,0:T(8,128)(2,1)S(1)}, bf16[2,128,256]{2,1,0:T(8,128)(2,1)S(1)}, u32[]{:S(2)}, u32[]{:S(2)}) collective-permute-start(bf16[2,128,256]{2,1,0:T(8,128)(2,1)S(1)} %get-tuple-element.5), channel_id=1, source_target_pairs={{0,256},{16,272},{32,288},{48,304},{64,320},{80,336},{96,352},{112... | collective-permute-start | bytes 393224 | tf_op jit(solution)/shard_map/ppermute | solution.py:15
  (5 other events, 625.7 us)
Sparse Core Ops, SparseCore 0:
  10.6 125.9 all-gather.1
  143.0 61.8 reduce-scatter.1
where the time goes:
time: 455 us; the launch traced here: 454 us
  waiting for transfers between devices  318 us (70%)
  starting transfers between devices  94.3 us (21%)
  matrix products  18.3 us (4%)
  between operations  14.6 us (3%)
  other arithmetic  7.06 us (2%)
    all_gather x1, waiting for transfers between devices, per_device(): lax.all_gather(in_weight, 'seq', axis=2, tiled=True)  129 us
    ppermute x21, waiting for transfers between devices, from_partner(): return lax.ppermute(value, axis, pairs)  124 us
    ppermute x21, starting transfers between devices, from_partner(): return lax.ppermute(value, axis, pairs)  89.8 us
    reduce_scatter x1, waiting for transfers between devices, per_device(): lax.psum_scatter(partial_sums.astype(jnp.bfloat16), 'chan', scatter_dimen...  62.1 us
  transfers between devices with their start and end apart: 24, of which 24 were waited for; matrix products, arithmetic and copies ran while one was open for 0% of the time, Pallas kernels for 0%

commit v1 on v0

v1 whole, which is shorter than its diff:
```python
import jax
import jax.numpy as jnp
import ml_dtypes
import numpy as np
from jax import lax
from jax.experimental import pallas as pl
from jax.experimental.pallas import tpu as pltpu
from jax.sharding import PartitionSpec as P

MESH = pl.DeviceIdType.MESH
F32 = jnp.float32
BF16 = jnp.bfloat16


def split_table(table):
    high = table.astype(ml_dtypes.bfloat16)
    low = (table - high.astype(np.float64)).astype(ml_dtypes.bfloat16)
    return np.stack([high, low])


def tables():
    row = np.arange(64)
    outer = 8 * (row % 8) + row // 8
    freq = np.arange(64) + 0.25
    lane = np.arange(128)
    chi = 2 * np.pi * np.outer(freq, outer) / 64
    phi = 2 * np.pi * np.outer(freq, lane) / 8192
    psi = 2 * np.pi * np.outer(lane, lane) / 128
    first = np.concatenate([np.cos(chi), -np.sin(chi)], 0)
    twist = np.stack([np.cos(phi), np.sin(phi)]).astype(np.float32)
    second = np.block([[np.cos(psi), -np.sin(psi)], [np.sin(psi), np.cos(psi)]])
    last = np.concatenate([np.cos(chi).T, -np.sin(chi).T], 1)
    return (
        split_table(first),
        twist,
        split_table(second),
        split_table(second.T),
        split_table(last),
    )


def split(value):
    high = value.astype(BF16)
    return high, (value - high.astype(F32)).astype(BF16)


def dot(left, right):
    return jnp.dot(left, right, preferred_element_type=F32)


def table_left(table, value):
    high, low = split(value)
    return dot(table[0], high) + (dot(table[0], low) + dot(table[1], high))


def table_right(value, table):
    high, low = split(value)
    return dot(high, table[0]) + (dot(low, table[0]) + dot(high, table[1]))


def kernel(
    tok_in, w_in, short_in, filt_in, skip_in, first, twist, second, second_t, last,
    out,
    tok, wstage, wbuf, sbuf, rbuf, sums, abuf, xbuf, xwide,
    fstage, fbuf, pstage, pbuf, spectrum, obuf, gbuf,
    tok_send, tok_recv, sib_send, sib_recv, wa_send, wa_recv, wr_send, wr_recv,
    x_send, x_recv, a_send, a_recv, f_send, f_recv, p_send, p_recv, o_send, o_recv,
):
    seq, chan = lax.axis_index("seq"), lax.axis_index("chan")
    y, zh = seq // 4, seq % 4
    x, zl, core = chan // 4, (chan // 2) % 2, chan % 2
    z = zh * 2 + zl

    def device(y_, zh_, x_, zl_, core_):
        return (y_ * 4 + zh_, (x_ * 2 + zl_) * 2 + core_)

    def device_z(z_):
        return device(y, z_ // 2, x, z_ % 2, core)

    sibling = device(y, zh, x, zl, 1 - core)
    mirrored = (zl == y // 4) & (core == zh // 2)

    def out_owner(i):
        return device(i // 4, i % 4, x, y // 4, zh // 2)

    def filter_owner(i):
        return device(4 * zl + i % 4, 2 * core + i // 16, x, (i // 8) % 2, (i // 4) % 2)

    barrier = pltpu.get_barrier_semaphore()

    def greet(target):
        pl.semaphore_signal(barrier, inc=1, device_id=target, device_id_type=MESH)

    greet(device_z((z + 1) % 8))
    greet(device_z((z + 7) % 8))
    for delta in range(1, 4):
        mate = (zl * 2 + core + delta) % 4
        greet(device(y, zh, x, mate // 2, mate % 2))
        greet(device(y, zh, (x + delta) % 4, zl, core))
    for delta in range(1, 8):
        greet(device((y + delta) % 8, zh, x, zl, core))

    own_out = seq
    own_filter = (zh % 2) * 16 + zl * 8 + core * 4 + y % 4

    @pl.loop(0, 32)
    def _(i):
        @pl.when(jnp.logical_not(mirrored & (i == own_out)))
        def _():
            greet(out_owner(i))

        @pl.when(jnp.logical_not(mirrored & (i == own_filter)))
        def _():
            greet(filter_owner(i))

    for c in range(2):
        tok[z, core, c] = tok_in[c * 128 : (c + 1) * 128, :]
    for b in range(3):
        turned = jnp.transpose(w_in[b], (1, 0))
        for q in range(4):
            wstage[q, b * 16 : (b + 1) * 16, :] = turned[q * 16 : (q + 1) * 16, :]
    for j in range(2):
        fstage[pl.ds(j, 128, stride=2), :] = filt_in[:, j * 128 : (j + 1) * 128]
    pstage[...] = jnp.zeros_like(pstage)
    for i in range(3):
        for b in range(3):
            pstage[i * 3 + b : i * 3 + b + 1, :] = short_in[i, b : b + 1, :]
    pstage[9:10, :] = skip_in[...]

    pl.semaphore_wait(barrier, 79 - 2 * mirrored.astype(jnp.int32))

    def remote(src, dst, send, recv, target):
        return pltpu.make_async_remote_copy(
            src_ref=src, dst_ref=dst, send_sem=send, recv_sem=recv,
            device_id=target, device_id_type=MESH,
        )

    def tok_step(way, d, c):
        shard = (z - (d - 1)) % 8 if way == 0 else (z + (d - 1)) % 8
        target = device_z((z + 1) % 8 if way == 0 else (z + 7) % 8)
        ref = tok.at[shard, core, c]
        return remote(
            ref, ref, tok_send.at[way, d - 1, c], tok_recv.at[way, d - 1, c], target
        )

    def sib_step(slot, c):
        ref = tok.at[(z - slot) % 8, core, c]
        return remote(ref, ref, sib_send.at[slot, c], sib_recv.at[slot, c], sibling)

    def w_step(way, d, c):
        shard = (y - (d - 1)) % 8 if way == 0 else (y + (d - 1)) % 8
        target = device((y + 1) % 8 if way == 0 else (y + 7) % 8, zh, x, zl, core)
        ref = wbuf.at[shard, c]
        return remote(
            ref, ref, wr_send.at[way, d - 1, c], wr_recv.at[way, d - 1, c], target
        )

    def goes(d, way, c):
        return d < 4 or way == c

    for c in range(2):
        for way in range(2):
            tok_step(way, 1, c).start()
        sib_step(0, c).start()

    quarter = zl * 2 + core

    def wa_step(delta):
        mate = (quarter + delta) % 4
        return remote(
            wstage.at[mate], wbuf.at[y, zl, core], wa_send.at[delta], wa_recv.at[delta],
            device(y, zh, x, mate // 2, mate % 2),
        )

    for delta in range(1, 4):
        wa_step(delta).start()
    wbuf[y, zl, core] = wstage[quarter]

    def f_step(i):
        return remote(
            fstage.at[pl.ds(pl.multiple_of(i * 8, 8), 8)], fbuf.at[pl.ds(pl.multiple_of(seq * 8, 8), 8)],
            f_send.at[i], f_recv.at[0], filter_owner(i),
        )

    def f_local():
        return pltpu.make_async_copy(
            fstage.at[pl.ds(pl.multiple_of(own_filter * 8, 8), 8)],
            fbuf.at[pl.ds(pl.multiple_of(seq * 8, 8), 8)], f_recv.at[0],
        )

    def p_step(delta):
        mate = (quarter + delta) % 4
        return remote(
            pstage, pbuf, p_send.at[delta], p_recv.at[0], device(y, zh, x, mate // 2, mate % 2)
        )

    @pl.loop(0, 32)
    def _(i):
        @pl.when(jnp.logical_not(mirrored & (i == own_filter)))
        def _():
            f_step(i).start()

    @pl.when(mirrored)
    def _():
        f_local().start()
        pltpu.make_async_copy(pstage, pbuf, p_recv.at[0]).start()
        for delta in range(1, 4):
            p_step(delta).start()

    for delta in range(1, 4):
        wa_step(delta).wait_recv()
    for c in range(2):
        for way in range(2):
            w_step(way, 1, c).start()

    def pass_tokens(d, c):
        for way in range(2):
            if goes(d, way, c):
                tok_step(way, d, c).wait_recv()
                if d < 4 and goes(d + 1, way, c):
                    tok_step(way, d + 1, c).start()
                sib_step(d if way == 0 else 8 - d, c).start()

    def pass_weights(d, c):
        for way in range(2):
            if goes(d, way, c):
                w_step(way, d, c).wait_recv()
                if d < 4 and goes(d + 1, way, c):
                    w_step(way, d + 1, c).start()

    def await_sibling(d):
        for c in range(2):
            for way in range(2):
                if goes(d, way, c) and (d > 0 or way == 0):
                    sib_step(0 if d == 0 else (d if way == 0 else 8 - d), c).wait_recv()

    sign = 2 * zl - 1
    blocks = [zh, (zh + sign) % 4, (zh - sign) % 4, (zh + 2) % 4]
    near = [[0], [1, 7], [2, 6], [3, 5], [4]]

    def x_step(p, row):
        return remote(
            sbuf.at[p, row], rbuf.at[p, x, row % 2], x_send.at[p, row], x_recv.at[p],
            device(y, zh, row // 2, zl, core),
        )

    def project(p, steps):
        rows = [(y + delta) % 8 for step in steps for delta in near[step]]
        total = jnp.zeros((48 * len(rows), 256), F32)
        for half in range(2):
            for side in range(2):
                left = jnp.concatenate([wbuf[row, half, side] for row in rows], 0)
                right = tok[blocks[p] * 2 + half, side].reshape(256, 512)
                total = total + lax.dot_general(
                    left, right, (((1,), (1,)), ((), ())), preferred_element_type=F32
                )
        rounded = total.astype(BF16)
        for n, row in enumerate(rows):
            sbuf[p, row] = rounded[n * 48 : (n + 1) * 48, :]
        for row in rows:
            @pl.when(row // 2 != x)
            def _():
                x_step(p, row).start()

            @pl.when(row // 2 == x)
            def _():
                pltpu.make_async_copy(
                    sbuf.at[p, row], rbuf.at[p, x, row % 2], x_recv.at[p]
                ).start()

    def a_step(p, delta):
        target = (y + delta) % 8
        return remote(
            abuf.at[p, target], xbuf.at[blocks[p], y], a_send.at[p, delta], a_recv.at[p],
            device(target, zh, x, zl, core),
        )

    def reduce(p):
        pltpu.make_async_copy(rbuf.at[p], rbuf.at[p], x_recv.at[p]).wait()
        total = rbuf[p, 0].astype(F32)
        for n in range(1, 4):
            total = total + rbuf[p, n].astype(F32)
        total = total.reshape(96, 256)
        for j in range(2):
            sums[pl.ds(j, 96, stride=2), :] = total[:, j * 128 : (j + 1) * 128]
        for target in range(8):
            first_row = (target // 4) * 96 + (target % 4) * 8
            parts = [sums[first_row + b * 32 : first_row + b * 32 + 8, :] for b in range(3)]
            parts.append(jnp.zeros((8, 128), F32))
            abuf[p, target] = jnp.concatenate(parts, 0).astype(BF16)
        for delta in range(1, 8):
            a_step(p, delta).start()
        pltpu.make_async_copy(abuf.at[p, y], xbuf.at[blocks[p], y], a_recv.at[p]).start()

    def transform(value):
        stage = table_left(first, value)
        rows = []
        for ch in range(4):
            re = stage[:64, ch * 128 : (ch + 1) * 128]
            im = stage[64:, ch * 128 : (ch + 1) * 128]
            rows.append(
                jnp.concatenate(
                    [re * twist[0] + im * twist[1], im * twist[0] - re * twist[1]], 1
                )
            )
        return table_right(jnp.concatenate(rows, 0), second)

    pass_tokens(1, 0)
    pass_weights(1, 0)
    pass_tokens(1, 1)

    pltpu.make_async_copy(fbuf, fbuf, f_recv.at[0]).wait()
    pltpu.make_async_copy(pbuf, pbuf, p_recv.at[0]).wait()
    lanes = []
    for ch in range(4):
        lanes.append(
            jnp.concatenate(
                [
                    fbuf[pl.ds((inner // 2) * 8 + ch * 2 + inner % 2, 8, stride=32), :]
                    for inner in range(8)
                ],
                0,
            )
        )
    spectrum[...] = transform(jnp.concatenate(lanes, 1)) * (1.0 / 8192.0)

    pass_weights(1, 1)
    await_sibling(0)
    await_sibling(1)
    project(0, [0, 1])
    pass_tokens(2, 0)
    pass_weights(2, 0)
    pass_tokens(2, 1)
    pass_weights(2, 1)
    await_sibling(2)
    project(0, [2])
    project(1, [0, 1, 2])
    pass_weights(3, 0)
    pass_tokens(3, 0)
    pass_weights(3, 1)
    project(0, [3])
    project(1, [3])
    pass_tokens(3, 1)
    await_sibling(3)
    project(2, [0, 1, 2, 3])
    for c in range(2):
        pass_weights(4, c)
    project(0, [4])
    project(1, [4])
    project(2, [4])
    reduce(0)
    for c in range(2):
        pass_tokens(4, c)
    await_sibling(4)
    project(3, [0, 1, 2, 3, 4])
    reduce(1)
    reduce(2)
    reduce(3)

    channel = 64 * (zh % 2) + 32 * zl + 16 * core + 4 * (y % 4)
    lane_at = lax.broadcasted_iota(jnp.int32, (16, 128), 1)
    gains = [
        jnp.sum(jnp.where(lane_at == channel + ch, pbuf[...], 0.0), axis=1, keepdims=True)
        for ch in range(4)
    ]
    for p in range(4):
        pltpu.make_async_copy(xbuf.at[blocks[p]], xbuf.at[blocks[p]], a_recv.at[p]).wait()
    xwide[...] = xbuf[...].astype(F32).reshape(1024, 128)
    lane = lax.broadcasted_iota(jnp.int32, (64, 128), 1)
    below = lax.broadcasted_iota(jnp.int32, (8, 128), 0)

    def mixed(b, ch):
        here = jnp.concatenate(
            [
                xwide[pl.ds((inner // 2) * 256 + (b * 4 + ch) * 2 + inner % 2, 8, stride=32), :]
                for inner in range(8)
            ],
            0,
        )
        total = gains[ch][b : b + 1, :] * here
        for i in range(1, 3):
            turned = pltpu.roll(here, i, 1)
            wrapped = jnp.where(below == 0, 0.0, pltpu.roll(turned[56:, :], 1, 0))
            before = jnp.concatenate([wrapped, turned[:56, :]], 0)
            total = total + gains[ch][i * 3 + b : i * 3 + b + 1, :] * jnp.where(
                lane < i, before, turned
            )
        return total

    drives = [mixed(1, ch) * mixed(2, ch) for ch in range(4)]
    wave = transform(jnp.concatenate(drives, 1))
    wave_re, wave_im = wave[:, :128], wave[:, 128:]
    filt_re, filt_im = spectrum[:, :128], spectrum[:, 128:]
    product = jnp.concatenate(
        [wave_re * filt_re - wave_im * filt_im, wave_re * filt_im + wave_im * filt_re], 1
    )
    back = table_right(product, second_t)
    columns = []
    for ch in range(4):
        re = back[ch * 64 : (ch + 1) * 64, :128]
        im = back[ch * 64 : (ch + 1) * 64, 128:]
        columns.append(
            jnp.concatenate(
                [re * twist[0] - im * twist[1], im * twist[0] + re * twist[1]], 0
            )
        )
    convolved = table_left(last, jnp.concatenate(columns, 1))
    for ch in range(4):
        gated = mixed(0, ch) * (
            convolved[:, ch * 128 : (ch + 1) * 128] + gains[ch][9:10, :] * drives[ch]
        )
        for inner in range(8):
            obuf[pl.ds((inner // 2) * 8 + ch * 2 + inner % 2, 8, stride=32), :] = gated[
                inner * 8 : (inner + 1) * 8, :
            ]

    def o_step(i):
        return remote(
            obuf.at[pl.ds(pl.multiple_of(i * 8, 8), 8)],
            gbuf.at[pl.ds(pl.multiple_of(own_filter * 8, 8), 8)],
            o_send.at[i], o_recv.at[0], out_owner(i),
        )

    @pl.loop(0, 32)
    def _(i):
        @pl.when(jnp.logical_not(mirrored & (i == own_out)))
        def _():
            o_step(i).start()

    @pl.when(mirrored)
    def _():
        pltpu.make_async_copy(
            obuf.at[pl.ds(pl.multiple_of(own_out * 8, 8), 8)],
            gbuf.at[pl.ds(pl.multiple_of(own_filter * 8, 8), 8)], o_recv.at[0],
        ).start()

    for d in range(1, 5):
        for c in range(2):
            for way in range(2):
                if goes(d, way, c):
                    tok_step(way, d, c).wait_send()
                    w_step(way, d, c).wait_send()
                    sib_step(d if way == 0 else 8 - d, c).wait_send()
    for c in range(2):
        sib_step(0, c).wait_send()
    for delta in range(1, 4):
        wa_step(delta).wait_send()
    for p in range(4):
        for row in range(8):
            @pl.when(row // 2 != x)
            def _():
                x_step(p, row).wait_send()
        for delta in range(1, 8):
            a_step(p, delta).wait_send()

    @pl.when(mirrored)
    def _():
        for delta in range(1, 4):
            p_step(delta).wait_send()

    @pl.loop(0, 32)
    def _(i):
        @pl.when(jnp.logical_not(mirrored & (i == own_filter)))
        def _():
            f_step(i).wait_send()

        @pl.when(jnp.logical_not(mirrored & (i == own_out)))
        def _():
            o_step(i).wait_send()

    pltpu.make_async_copy(gbuf, gbuf, o_recv.at[0]).wait()
    for j in range(2):
        out[:, j * 128 : (j + 1) * 128] = gbuf[pl.ds(j, 128, stride=2), :].astype(BF16)


def per_device(tokens, in_weight, short_filter, long_filter, skip_gain):
    consts = [jnp.asarray(table) for table in tables()]
    dma = pltpu.SemaphoreType.DMA
    vmem = pl.BlockSpec(memory_space=pltpu.VMEM)
    return pl.pallas_call(
        kernel,
        out_shape=jax.ShapeDtypeStruct((128, 256), BF16),
        in_specs=[vmem] * 10,
        out_specs=vmem,
        scratch_shapes=[
            pltpu.VMEM((8, 2, 2, 128, 512), BF16),
            pltpu.VMEM((4, 48, 512), BF16),
            pltpu.VMEM((8, 2, 2, 48, 512), BF16),
            pltpu.VMEM((4, 8, 48, 256), BF16),
            pltpu.VMEM((4, 4, 2, 48, 256), BF16),
            pltpu.VMEM((192, 128), F32),
            pltpu.VMEM((4, 8, 32, 128), BF16),
            pltpu.VMEM((4, 8, 32, 128), BF16),
            pltpu.VMEM((1024, 128), F32),
            pltpu.VMEM((256, 128), F32),
            pltpu.VMEM((256, 128), F32),
            pltpu.VMEM((16, 128), F32),
            pltpu.VMEM((16, 128), F32),
            pltpu.VMEM((256, 256), F32),
            pltpu.VMEM((256, 128), F32),
            pltpu.VMEM((256, 128), F32),
            dma((2, 4, 2)), dma((2, 4, 2)),
            dma((8, 2)), dma((8, 2)),
            dma((4,)), dma((4,)),
            dma((2, 4, 2)), dma((2, 4, 2)),
            dma((4, 8)), dma((4,)),
            dma((4, 8)), dma((4,)),
            dma((32,)), dma((1,)),
            dma((4,)), dma((1,)),
            dma((32,)), dma((1,)),
        ],
        compiler_params=pltpu.CompilerParams(
            collective_id=0, has_side_effects=True, vmem_limit_bytes=40 * 1024 * 1024
        ),
    )(tokens, in_weight, short_filter, long_filter, skip_gain[None, :], *consts)


def solution(mesh):
    placed = (
        P("seq", "chan"),
        P(None, "chan", "seq"),
        P(None, None, "chan"),
        P("chan", "seq"),
        P("chan"),
    )
    return jax.shard_map(
        per_device, mesh=mesh, in_specs=placed, out_specs=P("chan", "seq"), check_vma=False
    )
```

time: 455 us -> 83 us (0.18)
  the two profiles are of different devices: /device:TPU:6 before, /device:TPU:1 now
where the time goes in v1:
time: 83 us; the launch traced here: 82.6 us
  Pallas kernels  75.9 us (91%)
  local copies, waits for them, and re-layouts  6.64 us (8%)
    pallas_call x1, Pallas kernels, per_device(): pl.pallas_call(kernel, out_shape=jax.ShapeDtypeStruct((128, 256), BF16),...  75.9 us
    unnamed x20, local copies, waits for them, and re-layouts  6.64 us

profile of v1, /device:TPU:1, one launch (start us, length us, event | category | flops | bytes accessed | tf_op | source)
XLA Modules:
  0.0 82.6 jit_solution(13333488701982371298)
XLA Ops:
  0.0 0.0 copy-start
  0.0 0.0 copy-start.1
  0.0 0.0 copy-start.4
  0.0 1.2 %copy.11.w_in = bf16[3,512,64]{2,1,0:T(8,128)(2,1)S(1)} copy(bf16[3,512,64]{1,2,0:T(8,128)(2,1)} %param.11) | data formatting | bytes 393216 | tf_op args[1]
  1.2 0.0 copy-done
  1.2 0.0 copy-done.1
  1.2 0.0 copy-done.4
  1.3 0.0 copy-start.2
  1.3 0.9 %copy-done.2 = bf16[2,256,256]{2,1,0:T(8,128)(2,1)S(1)} copy-done((bf16[2,256,256]{2,1,0:T(8,128)(2,1)S(1)}, bf16[2,256,256]{2,1,0:T(8,128)(2,1)}, u32[]{:S(2)}) %copy-start.2) | copy-done | bytes 262168
  2.2 0.0 copy-start.3
  2.2 0.9 %copy-done.3 = f32[128,256]{1,0:T(8,128)S(1)} copy-done((f32[128,256]{1,0:T(8,128)S(1)}, f32[128,256]{1,0:T(8,128)}, u32[]{:S(2)}) %copy-start.3) | copy-done | bytes 131096
  3.1 0.0 copy-start.5
  3.1 0.8 %copy-done.5 = bf16[2,128,64]{2,1,0:T(8,128)(2,1)S(1)} copy-done((bf16[2,128,64]{2,1,0:T(8,128)(2,1)S(1)}, bf16[2,128,64]{2,1,0:T(8,128)(2,1)}, u32[]{:S(2)}) %copy-start.5) | copy-done | bytes 32792
  4.0 0.0 copy-start.6
  4.0 0.8 copy-done.6
  4.7 0.0 copy-start.7
  4.7 0.7 copy-done.7
  5.4 0.0 copy-start.8
  5.4 0.7 copy-done.8
  6.1 75.9 %shard_map.100 = bf16[128,256]{1,0:T(8,128)(2,1)S(1)} custom-call(bf16[256,512]{1,0:T(8,128)(2,1)S(1)} %copy-done, bf16[3,512,64]{2,1,0:T(8,128)(2,1)S(1)} %copy.11.w_in, f32[3,3,128]{2,1,0:T(4,128)S(1)} %copy-done.7, f32[128,256]{1,0:T(8,128)S(1)} %copy-done.3, f32[1,128]{1,0:T(1,128)S(1)} %bitcast.1, bf16[2,128,64]{2,1,0:T(8,128)(2,1)S(1)} %copy-done.5, ...), custom_call_target="tpu_custom_call" | custom-call | tf_op jit(solution)/shard_map/pallas_call | solution.py:480
  82.0 0.6 copy.13
Async XLA Ops:
  0.0 1.2 %copy-start = (bf16[256,512]{1,0:T(8,128)(2,1)S(1)}, bf16[256,512]{1,0:T(8,128)(2,1)}, u32[]{:S(2)}) copy-start(bf16[256,512]{1,0:T(8,128)(2,1)} %tok_in.1) | copy-start | bytes 786436
  0.0 1.2 %copy-start.1 = (bf16[2,256,256]{2,1,0:T(8,128)(2,1)S(1)}, bf16[2,256,256]{2,1,0:T(8,128)(2,1)}, u32[]{:S(2)}) copy-start(bf16[2,256,256]{2,1,0:T(8,128)(2,1)} %constant.13.clone.second_t) | copy-start | bytes 786436
  0.0 1.2 %copy-start.4 = (f32[2,64,128]{2,1,0:T(8,128)S(1)}, f32[2,64,128]{2,1,0:T(8,128)}, u32[]{:S(2)}) copy-start(f32[2,64,128]{2,1,0:T(8,128)} %constant.11.clone.twist) | copy-start | bytes 196612
  1.3 1.0 %copy-start.2 = (bf16[2,256,256]{2,1,0:T(8,128)(2,1)S(1)}, bf16[2,256,256]{2,1,0:T(8,128)(2,1)}, u32[]{:S(2)}) copy-start(bf16[2,256,256]{2,1,0:T(8,128)(2,1)} %constant.12.clone.second) | copy-start | bytes 786436
  2.2 0.9 %copy-start.3 = (f32[128,256]{1,0:T(8,128)S(1)}, f32[128,256]{1,0:T(8,128)}, u32[]{:S(2)}) copy-start(f32[128,256]{1,0:T(8,128)} %filt_in.1) | copy-start | bytes 393220
  3.1 0.8 %copy-start.5 = (bf16[2,128,64]{2,1,0:T(8,128)(2,1)S(1)}, bf16[2,128,64]{2,1,0:T(8,128)(2,1)}, u32[]{:S(2)}) copy-start(bf16[2,128,64]{2,1,0:T(8,128)(2,1)} %constant.10.clone.first) | copy-start | bytes 98308
  4.0 0.8 copy-start.6
  4.7 0.7 copy-start.7
  5.4 0.7 copy-start.8

commit v2 on v1

v2 whole, which is shorter than its diff:
```python
import jax
import jax.numpy as jnp
import numpy as np
from jax import lax
from jax.experimental import pallas as pl
from jax.experimental.pallas import tpu as pltpu
from jax.sharding import PartitionSpec as P

MESH = pl.DeviceIdType.MESH
F32 = jnp.float32
BF16 = jnp.bfloat16


def tables():
    row = np.arange(64)
    outer = 8 * (row % 8) + row // 8
    freq = np.arange(64) + 0.25
    lane = np.arange(128)
    chi = 2 * np.pi * np.outer(freq, outer) / 64
    phi = 2 * np.pi * np.outer(freq, lane) / 8192
    psi = 2 * np.pi * np.outer(lane, lane) / 128
    first = np.concatenate([np.cos(chi), -np.sin(chi)], 0)
    twist = np.stack([np.cos(phi), np.sin(phi)]).astype(np.float32)
    second = np.block([[np.cos(psi), -np.sin(psi)], [np.sin(psi), np.cos(psi)]])
    last = np.concatenate([np.cos(chi).T, -np.sin(chi).T], 1)
    return (
        first.astype(np.float32),
        twist,
        second.astype(np.float32),
        last.astype(np.float32),
    )


def split(value):
    high = value.astype(BF16)
    return high, (value - high.astype(F32)).astype(BF16)


def dot(left, right):
    return jnp.dot(left, right, preferred_element_type=F32)


def table_left(table, value):
    table = split(table)
    high, low = split(value)
    return dot(table[0], high) + (dot(table[0], low) + dot(table[1], high))


def table_right(value, table):
    table = split(table)
    high, low = split(value)
    return dot(high, table[0]) + (dot(low, table[0]) + dot(high, table[1]))


def kernel(
    tok_in, w_in, short_in, filt_in, skip_in, first_in, twist_in, second_in, last_in,
    out,
    first, twist, second, last, short, skip, filt,
    tok, wown, wbuf, sbuf, rbuf, sums, aearly, xearly, alate, xlate, xwide,
    fstage, fmid, fwide, fturn, fbuf, pstage, pbuf, spectrum, oturn, omid, ostage,
    in_sem, tok_sem, own_sem, param_sem, table_sem,
    tok_send, tok_recv, sib_send, sib_recv, wa_send, wa_recv, wr_send, wr_recv,
    x_send, x_recv, e_send, e_recv, a_send, a_recv, f_send, f_recv, g_send, g_recv, p_send, p_recv,
    n_send, n_recv, o_send, o_recv,
):
    seq, chan = lax.axis_index("seq"), lax.axis_index("chan")
    y, zh = seq // 4, seq % 4
    x, zl, core = chan // 4, (chan // 2) % 2, chan % 2
    z = zh * 2 + zl

    def device(y_, zh_, x_, zl_, core_):
        return (y_ * 4 + zh_, (x_ * 2 + zl_) * 2 + core_)

    def device_z(z_):
        return device(y, z_ // 2, x, z_ % 2, core)

    sibling = device(y, zh, x, zl, 1 - core)
    mirrored = (zl == y // 4) & (core == zh // 2)

    def in_column(i):
        return device(y, i // 4, x, (i // 2) % 2, i % 2)

    def filter_holder(i):
        return device(y, 2 * core + i // 4, x, (i // 2) % 2, i % 2)

    def out_owner(i):
        return device(y, i % 4, x, i // 4, zh // 2)

    at_home = core == zh // 2
    own_block = (zh % 2) * 4 + zl * 2 + core
    own_out = zl * 4 + zh
    column_at = zh * 4 + zl * 2 + core

    barrier = pltpu.get_barrier_semaphore()

    def greet(target):
        pl.semaphore_signal(barrier, inc=1, device_id=target, device_id_type=MESH)

    @pl.loop(1, 16)
    def _(delta):
        greet(in_column((column_at + delta) % 16))

    for delta in range(1, 4):
        greet(device(y, zh, (x + delta) % 4, zl, core))

    @pl.loop(1, 8)
    def _(delta):
        greet(device((y + delta) % 8, zh, x, zl, core))

    quarter = zl * 2 + core
    own_tok = pltpu.make_async_copy(tok_in, tok.at[z, core], tok_sem.at[0])
    own_w = pltpu.make_async_copy(w_in, wown, own_sem.at[0])
    own_filt = pltpu.make_async_copy(filt_in, filt, in_sem.at[0])
    own_params = [
        pltpu.make_async_copy(short_in, short, param_sem.at[0]),
        pltpu.make_async_copy(skip_in, skip, param_sem.at[1]),
    ]
    own_tables = [
        pltpu.make_async_copy(first_in, first, table_sem.at[0]),
        pltpu.make_async_copy(twist_in, twist, table_sem.at[1]),
        pltpu.make_async_copy(second_in, second, table_sem.at[2]),
        pltpu.make_async_copy(last_in, last, table_sem.at[3]),
    ]
    for copy in [own_tok, own_w, own_filt] + own_params + own_tables:
        copy.start()

    pl.semaphore_wait(barrier, 25)

    def remote(src, dst, send, recv, target):
        return pltpu.make_async_remote_copy(
            src_ref=src, dst_ref=dst, send_sem=send, recv_sem=recv,
            device_id=target, device_id_type=MESH,
        )

    def tok_step(way, d, c):
        shard = (z - (d - 1)) % 8 if way == 0 else (z + (d - 1)) % 8
        target = device_z((z + 1) % 8 if way == 0 else (z + 7) % 8)
        ref = tok.at[shard, core, c]
        return remote(
            ref, ref, tok_send.at[way, d - 1, c], tok_recv.at[way, d - 1, c], target
        )

    def sib_step(slot, c):
        ref = tok.at[(z - slot) % 8, core, c]
        return remote(ref, ref, sib_send.at[slot, c], sib_recv.at[slot, c], sibling)

    def w_step(way, d, k):
        shard = (y - (d - 1)) % 8 if way == 0 else (y + (d - 1)) % 8
        target = device((y + 1) % 8 if way == 0 else (y + 7) % 8, zh, x, zl, core)
        ref = wbuf.at[shard, held(k)]
        return remote(
            ref, ref, wr_send.at[way, d - 1, k], wr_recv.at[way, d - 1, k], target
        )

    def held(k):
        flipped = core if k % 2 == 0 else 1 - core
        return (zl if k < 2 else 1 - zl) * 2 + flipped

    def goes(d, way, k):
        return d < 4 or k < 1

    def wa_step(k):
        mate = held(k)
        return remote(
            wown.at[:, mate], wbuf.at[y, quarter], wa_send.at[k], wa_recv.at[k],
            device(y, zh, x, mate // 2, mate % 2),
        )

    def ends(way, k):
        return k if way == 0 else 1 - k

    own_w.wait()
    for k in range(1, 4):
        wa_step(k).start()
    wbuf[y, quarter] = wown[:, quarter]
    own_tok.wait()
    for k in range(2):
        for way in range(2):
            if k == 0:
                w_step(way, 1, 0).start()
            tok_step(way, 1, ends(way, k)).start()
    for c in range(2):
        sib_step(0, c).start()

    own_filt.wait()
    fstage[...] = filt[...].astype(BF16)
    for copy in own_params:
        copy.wait()
    pstage[...] = jnp.zeros_like(pstage)
    for i in range(3):
        for b in range(3):
            pstage[i * 3 + b : i * 3 + b + 1, :] = short[i, b : b + 1, :]
    pstage[9:10, :] = skip[...]

    def f_step(i):
        return remote(
            fstage.at[pl.ds(i * 16, 16)], fmid.at[zl, zh], f_send.at[i], f_recv.at[0],
            filter_holder(i),
        )

    def g_step(delta):
        target = (y + delta) % 8
        return remote(
            fturn.at[target], fbuf.at[y], g_send.at[delta], g_recv.at[0],
            device(target, zh, x, zl, core),
        )

    def p_step(delta):
        mate = (quarter + delta) % 4
        return remote(
            pstage, pbuf, p_send.at[delta], p_recv.at[0], device(y, zh, x, mate // 2, mate % 2)
        )

    for i in range(8):
        @pl.when(jnp.logical_not(at_home & (own_block == i)))
        def _():
            f_step(i).start()

    @pl.when(at_home)
    def _():
        pltpu.make_async_copy(
            fstage.at[pl.ds(pl.multiple_of(own_block * 16, 16), 16)], fmid.at[zl, zh],
            f_recv.at[0],
        ).start()

    @pl.when(mirrored)
    def _():
        pltpu.make_async_copy(pstage, pbuf, p_recv.at[0]).start()
        for delta in range(1, 4):
            p_step(delta).start()

    for k in range(1, 4):
        wa_step(k).wait_recv()
        for way in range(2):
            w_step(way, 1, k).start()

    def pass_tokens(d, k):
        for way in range(2):
            c = ends(way, k)
            tok_step(way, d, c).wait_recv()
            if d < 4 and goes(d + 1, way, k):
                tok_step(way, d + 1, c).start()
            sib_step(d if way == 0 else 8 - d, c).start()

    def pass_weights(d, k):
        for way in range(2):
            if d < 4 or k // 2 == way:
                w_step(way, d, k).wait_recv()
                if d < 3 or (d == 3 and k // 2 == way):
                    w_step(way, d + 1, k).start()

    def await_sibling(d):
        for half in range(2):
            for way in range(2):
                if (0 < d < 4) or (d == 0 and way == 0) or (d == 4 and half == way):
                    sib_step(0 if d == 0 else (d if way == 0 else 8 - d), half).wait_recv()

    sign = 2 * zl - 1
    blocks = [zh, (zh + sign) % 4, (zh - sign) % 4, (zh + 2) % 4]
    near = [[0], [1, 7], [2, 6], [3, 5], [4]]

    def x_step(p, row):
        return remote(
            sbuf.at[p, row], rbuf.at[p, x, row % 2], x_send.at[p, row], x_recv.at[p],
            device(y, zh, row // 2, zl, core),
        )

    def project(p, steps):
        rows = [(y + delta) % 8 for step in steps for delta in near[step]]
        total = jnp.zeros((48 * len(rows), 256), F32)
        for half in range(2):
            for side in range(2):
                left = jnp.concatenate([wbuf[row, half * 2 + side].reshape(48, 512) for row in rows], 0)
                right = tok[blocks[p] * 2 + half, side].reshape(256, 512)
                total = total + lax.dot_general(
                    left, right, (((1,), (1,)), ((), ())), preferred_element_type=F32
                )
        rounded = total.astype(BF16)
        for n, row in enumerate(rows):
            sbuf[p, row] = rounded[n * 48 : (n + 1) * 48, :]
        for row in rows:
            @pl.when(row // 2 != x)
            def _():
                x_step(p, row).start()

            @pl.when(row // 2 == x)
            def _():
                pltpu.make_async_copy(
                    sbuf.at[p, row], rbuf.at[p, x, row % 2], x_recv.at[p]
                ).start()

    def sum_over_x(p):
        pltpu.make_async_copy(rbuf.at[p], rbuf.at[p], x_recv.at[p]).wait()
        total = rbuf[p, 0].astype(F32)
        for n in range(1, 4):
            total = total + rbuf[p, n].astype(F32)
        total = total.reshape(96, 256)
        for j in range(2):
            sums[p, pl.ds(j, 96, stride=2), :] = total[:, j * 128 : (j + 1) * 128]

    def pieces(p, target):
        first_row = (target // 4) * 96 + (target % 4) * 8
        return [sums[p, first_row + b * 32 : first_row + b * 32 + 8, :] for b in range(3)]

    def e_step(delta):
        target = (y + delta) % 8
        return remote(
            aearly.at[target], xearly.at[y], e_send.at[delta], e_recv.at[0],
            device(target, zh, x, zl, core),
        )

    def a_step(delta):
        target = (y + delta) % 8
        return remote(
            alate.at[target], xlate.at[y], a_send.at[delta], a_recv.at[0],
            device(target, zh, x, zl, core),
        )

    padding = jnp.zeros((8, 128), F32)

    def reduce_early():
        for p in range(3):
            sum_over_x(p)
        for target in range(8):
            parts = pieces(0, target) + pieces(1, target) + pieces(2, target)
            aearly[target] = jnp.concatenate(parts + [padding], 0).astype(BF16)
        for delta in range(1, 8):
            e_step(delta).start()
        pltpu.make_async_copy(aearly.at[y], xearly.at[y], e_recv.at[0]).start()

    def reduce_late():
        sum_over_x(3)
        for target in range(8):
            alate[target] = jnp.concatenate(pieces(3, target) + [padding], 0).astype(BF16)
        for delta in range(1, 8):
            a_step(delta).start()
        pltpu.make_async_copy(alate.at[y], xlate.at[y], a_recv.at[0]).start()

    def transform(value):
        stage = table_left(first[...], value)
        rows = []
        for ch in range(4):
            re = stage[:64, ch * 128 : (ch + 1) * 128]
            im = stage[64:, ch * 128 : (ch + 1) * 128]
            rows.append(
                jnp.concatenate(
                    [re * twist[0] + im * twist[1], im * twist[0] - re * twist[1]], 1
                )
            )
        return table_right(jnp.concatenate(rows, 0), second[...])

    pass_weights(1, 0)
    pass_tokens(1, 0)
    pass_weights(1, 1)
    pass_tokens(1, 1)
    pass_weights(1, 2)
    pass_weights(1, 3)
    await_sibling(0)
    await_sibling(1)
    pass_weights(2, 0)
    pass_tokens(2, 0)
    pass_weights(2, 1)
    project(0, [0, 1])
    pass_tokens(2, 1)
    pass_weights(2, 2)
    pass_weights(2, 3)

    pltpu.make_async_copy(fmid, fmid, f_recv.at[0]).wait()
    for side in range(2):
        for from_zh in range(4):
            piece = fmid[side, from_zh].astype(F32)
            for j in range(2):
                fwide[pl.ds(side * 128 + from_zh * 2 + j, 16, stride=8), :] = piece[
                    :, j * 128 : (j + 1) * 128
                ]
    fturn[...] = fwide[...].astype(BF16).reshape(8, 32, 128)
    for delta in range(1, 8):
        g_step(delta).start()
    pltpu.make_async_copy(fturn.at[y], fbuf.at[y], g_recv.at[0]).start()

    await_sibling(2)
    pass_weights(3, 0)
    pass_tokens(3, 0)
    pass_weights(3, 1)
    project(0, [2])
    project(1, [0, 1, 2])
    pass_tokens(3, 1)
    pass_weights(3, 2)
    pass_weights(3, 3)
    await_sibling(3)
    project(2, [0, 1, 2, 3])
    project(0, [3])
    project(1, [3])

    pltpu.make_async_copy(fbuf, fbuf, g_recv.at[0]).wait()
    pltpu.make_async_copy(pbuf, pbuf, p_recv.at[0]).wait()
    for copy in own_tables:
        copy.wait()
    fwide[...] = fbuf[...].astype(F32).reshape(256, 128)
    lanes = []
    for ch in range(4):
        lanes.append(
            jnp.concatenate(
                [fwide[pl.ds(ch * 8 + inner, 8, stride=32), :] for inner in range(8)], 0
            )
        )
    spectrum[...] = transform(jnp.concatenate(lanes, 1)) * (1.0 / 8192.0)

    for k in range(4):
        pass_weights(4, k)
    project(0, [4])
    project(1, [4])
    project(2, [4])
    pass_tokens(4, 0)
    await_sibling(4)
    project(3, [0, 1, 2, 3, 4])
    reduce_early()
    reduce_late()

    channel = 64 * (zh % 2) + 32 * zl + 16 * core + 4 * (y % 4)
    lane_at = lax.broadcasted_iota(jnp.int32, (16, 128), 1)
    gains = [
        jnp.sum(jnp.where(lane_at == channel + ch, pbuf[...], 0.0), axis=1, keepdims=True)
        for ch in range(4)
    ]
    pltpu.make_async_copy(xearly, xearly, e_recv.at[0]).wait()
    early = xearly[...].astype(F32)
    for p in range(3):
        xwide[blocks[p]] = early[:, p * 24 : (p + 1) * 24, :].reshape(192, 128)
    pltpu.make_async_copy(xlate, xlate, a_recv.at[0]).wait()
    xwide[blocks[3]] = xlate[...].astype(F32)[:, :24, :].reshape(192, 128)
    lane = lax.broadcasted_iota(jnp.int32, (64, 128), 1)
    below = lax.broadcasted_iota(jnp.int32, (8, 128), 0)

    def mixed(b, ch):
        here = jnp.concatenate(
            [
                xwide[inner // 2, pl.ds((b * 4 + ch) * 2 + inner % 2, 8, stride=24), :]
                for inner in range(8)
            ],
            0,
        )
        total = gains[ch][b : b + 1, :] * here
        for i in range(1, 3):
            turned = pltpu.roll(here, i, 1)
            wrapped = jnp.where(below == 0, 0.0, pltpu.roll(turned[56:, :], 1, 0))
            before = jnp.concatenate([wrapped, turned[:56, :]], 0)
            total = total + gains[ch][i * 3 + b : i * 3 + b + 1, :] * jnp.where(
                lane < i, before, turned
            )
        return total

    drives = [mixed(1, ch) * mixed(2, ch) for ch in range(4)]
    wave = transform(jnp.concatenate(drives, 1))
    wave_re, wave_im = wave[:, :128], wave[:, 128:]
    filt_re, filt_im = spectrum[:, :128], spectrum[:, 128:]
    product = jnp.concatenate(
        [wave_re * filt_re - wave_im * filt_im, wave_re * filt_im + wave_im * filt_re], 1
    )
    back = table_right(product, jnp.transpose(second[...], (1, 0)))
    columns = []
    for ch in range(4):
        re = back[ch * 64 : (ch + 1) * 64, :128]
        im = back[ch * 64 : (ch + 1) * 64, 128:]
        columns.append(
            jnp.concatenate(
                [re * twist[0] - im * twist[1], im * twist[0] + re * twist[1]], 0
            )
        )
    convolved = table_left(last[...], jnp.concatenate(columns, 1))
    for ch in range(4):
        gated = mixed(0, ch) * (
            convolved[:, ch * 128 : (ch + 1) * 128] + gains[ch][9:10, :] * drives[ch]
        )
        for inner in range(8):
            fwide[pl.ds(ch * 8 + inner, 8, stride=32), :] = gated[
                inner * 8 : (inner + 1) * 8, :
            ]

    oturn[...] = fwide[...].astype(BF16).reshape(8, 32, 128)

    def n_step(delta):
        target = (y + delta) % 8
        return remote(
            oturn.at[target], omid.at[y], n_send.at[delta], n_recv.at[0],
            device(target, zh, x, zl, core),
        )

    for delta in range(1, 8):
        n_step(delta).start()
    pltpu.make_async_copy(oturn.at[y], omid.at[y], n_recv.at[0]).start()

    out_rows = out.at[pl.ds(pl.multiple_of(own_block * 16, 16), 16)]

    def o_step(i):
        return remote(ostage.at[i], out_rows, o_send.at[i], o_recv.at[0], out_owner(i))

    pltpu.make_async_copy(omid, omid, n_recv.at[0]).wait()
    fwide[...] = omid[...].astype(F32).reshape(256, 128)
    for i in range(8):
        first_row = (i // 4) * 128 + (i % 4) * 2
        ostage[i] = jnp.concatenate(
            [fwide[pl.ds(first_row + j, 16, stride=8), :] for j in range(2)], 1
        ).astype(BF16)
    for i in range(8):
        @pl.when(jnp.logical_not(at_home & (own_out == i)))
        def _():
            o_step(i).start()

    @pl.when(at_home)
    def _():
        pltpu.make_async_copy(ostage.at[own_out], out_rows, o_recv.at[0]).start()

    for d in range(1, 5):
        for k in range(4):
            for way in range(2):
                if k < 2 and goes(d, way, k):
                    tok_step(way, d, ends(way, k)).wait_send()
                if d < 4 or k // 2 == way:
                    w_step(way, d, k).wait_send()
    for slot in range(8):
        for half in range(2):
            sib_step(slot, half).wait_send()
    for k in range(1, 4):
        wa_step(k).wait_send()
    for p in range(4):
        for row in range(8):
            @pl.when(row // 2 != x)
            def _():
                x_step(p, row).wait_send()

    @pl.when(mirrored)
    def _():
        for delta in range(1, 4):
            p_step(delta).wait_send()

    for i in range(8):
        @pl.when(jnp.logical_not(at_home & (own_block == i)))
        def _():
            f_step(i).wait_send()

        @pl.when(jnp.logical_not(at_home & (own_out == i)))
        def _():
            o_step(i).wait_send()

    for delta in range(1, 8):
        g_step(delta).wait_send()
        e_step(delta).wait_send()
        a_step(delta).wait_send()
        n_step(delta).wait_send()
    pltpu.make_async_copy(out, out, o_recv.at[0]).wait()


def per_device(tokens, in_weight, short_filter, long_filter, skip_gain):
    consts = [jnp.asarray(table) for table in tables()]
    dma = pltpu.SemaphoreType.DMA
    hbm = pl.BlockSpec(memory_space=pltpu.HBM)
    columns = jnp.transpose(in_weight, (0, 2, 1)).reshape(3, 4, 16, 512)
    return pl.pallas_call(
        kernel,
        out_shape=jax.ShapeDtypeStruct((128, 256), BF16),
        in_specs=[hbm] * 9,
        out_specs=hbm,
        scratch_shapes=[
            pltpu.VMEM((128, 64), F32),
            pltpu.VMEM((2, 64, 128), F32),
            pltpu.VMEM((256, 256), F32),
            pltpu.VMEM((64, 128), F32),
            pltpu.VMEM((3, 3, 128), F32),
            pltpu.VMEM((1, 128), F32),
            pltpu.VMEM((128, 256), F32),
            pltpu.VMEM((8, 2, 2, 128, 512), BF16),
            pltpu.VMEM((3, 4, 16, 512), BF16),
            pltpu.VMEM((8, 4, 3, 16, 512), BF16),
            pltpu.VMEM((4, 8, 48, 256), BF16),
            pltpu.VMEM((4, 4, 2, 48, 256), BF16),
            pltpu.VMEM((4, 192, 128), F32),
            pltpu.VMEM((8, 80, 128), BF16),
            pltpu.VMEM((8, 80, 128), BF16),
            pltpu.VMEM((8, 32, 128), BF16),
            pltpu.VMEM((8, 32, 128), BF16),
            pltpu.VMEM((4, 192, 128), F32),
            pltpu.VMEM((128, 256), BF16),
            pltpu.VMEM((2, 4, 16, 256), BF16),
            pltpu.VMEM((256, 128), F32),
            pltpu.VMEM((8, 32, 128), BF16),
            pltpu.VMEM((8, 32, 128), BF16),
            pltpu.VMEM((16, 128), F32),
            pltpu.VMEM((16, 128), F32),
            pltpu.VMEM((256, 256), F32),
            pltpu.VMEM((8, 32, 128), BF16),
            pltpu.VMEM((8, 32, 128), BF16),
            pltpu.VMEM((8, 16, 256), BF16),
            dma((1,)), dma((1,)), dma((1,)), dma((2,)), dma((4,)),
            dma((2, 4, 2)), dma((2, 4, 2)),
            dma((8, 2)), dma((8, 2)),
            dma((4,)), dma((4,)),
            dma((2, 4, 4)), dma((2, 4, 4)),
            dma((4, 8)), dma((4,)),
            dma((8,)), dma((1,)),
            dma((8,)), dma((1,)),
            dma((8,)), dma((1,)),
            dma((8,)), dma((1,)),
            dma((4,)), dma((1,)),
            dma((8,)), dma((1,)),
            dma((8,)), dma((1,)),
        ],
        compiler_params=pltpu.CompilerParams(
            collective_id=0, has_side_effects=True, vmem_limit_bytes=63 * 1024 * 1024
        ),
    )(tokens.reshape(2, 128, 512), columns, short_filter, long_filter, skip_gain[None, :], *consts)


def solution(mesh):
    placed = (
        P("seq", "chan"),
        P(None, "chan", "seq"),
        P(None, None, "chan"),
        P("chan", "seq"),
        P("chan"),
    )
    return jax.shard_map(
        per_device, mesh=mesh, in_specs=placed, out_specs=P("chan", "seq"), check_vma=False
    )
```

time: 83 us -> 71.1 us (0.86)
  Pallas kernels: 75.9 us -> 69.5 us
  local copies, waits for them, and re-layouts: 6.64 us -> 1.47 us
    pallas_call x1, Pallas kernels: 75.9 us -> 69.5 us  [per_device(): pl.pallas_call(kernel, out_shape=jax.ShapeDtypeStruct((128, 256), BF16),...]
    unnamed x20 -> x1, local copies, waits for them, and re-layouts: 6.64 us -> 1.47 us
where the time goes in v2:
time: 71.1 us; the launch traced here: 70.9 us
  Pallas kernels  69.5 us (98%)
  local copies, waits for them, and re-layouts  1.47 us (2%)
    pallas_call x1, Pallas kernels, per_device(): pl.pallas_call(kernel, out_shape=jax.ShapeDtypeStruct((128, 256), BF16),...  69.5 us
    unnamed x1, local copies, waits for them, and re-layouts  1.47 us

profile of v2, /device:TPU:1, one launch (start us, length us, event | category | flops | bytes accessed | tf_op | source)
XLA Modules:
  0.0 70.9 jit_solution(13702133141695964747)
XLA Ops:
  0.0 69.5 %shard_map.91 = bf16[128,256]{1,0:T(8,128)(2,1)} custom-call(bf16[2,128,512]{2,1,0:T(8,128)(2,1)} %bitcast.5, bf16[3,4,16,512]{3,2,1,0:T(8,128)(2,1)} %bitcast.6, f32[3,3,128]{2,1,0:T(4,128)} %short_in.1, f32[128,256]{1,0:T(8,128)} %filt_in.1, f32[1,128]{1,0:T(1,128)} %bitcast.7, f32[128,64]{1,0:T(8,128)} %constant.8.clone.first_in, ...), custom_call_target="tpu_custom_call" | custom-call | tf_op jit(solution)/shard_map/pallas_call | solution.py:559
  69.5 1.5 %copy.11 = bf16[128,256]{1,0:T(8,128)(2,1)} copy(bf16[128,256]{1,0:T(8,128)(2,1)} %shard_map.91) | data formatting | bytes 131072

commit v3 on v2

--- a/solution.py
+++ b/solution.py
@@ -77,9 +77,6 @@
     sibling = device(y, zh, x, zl, 1 - core)
     mirrored = (zl == y // 4) & (core == zh // 2)
 
-    def in_column(i):
-        return device(y, i // 4, x, (i // 2) % 2, i % 2)
-
     def filter_holder(i):
         return device(y, 2 * core + i // 4, x, (i // 2) % 2, i % 2)
 
@@ -89,23 +86,20 @@
     at_home = core == zh // 2
     own_block = (zh % 2) * 4 + zl * 2 + core
     own_out = zl * 4 + zh
-    column_at = zh * 4 + zl * 2 + core
 
     barrier = pltpu.get_barrier_semaphore()
 
     def greet(target):
         pl.semaphore_signal(barrier, inc=1, device_id=target, device_id_type=MESH)
 
-    @pl.loop(1, 16)
-    def _(delta):
-        greet(in_column((column_at + delta) % 16))
-
+    greet(device_z((z + 1) % 8))
+    greet(device_z((z + 7) % 8))
+    greet(device((y + 1) % 8, zh, x, zl, core))
+    greet(device((y + 7) % 8, zh, x, zl, core))
     for delta in range(1, 4):
+        mate = (zl * 2 + core + delta) % 4
+        greet(device(y, zh, x, mate // 2, mate % 2))
         greet(device(y, zh, (x + delta) % 4, zl, core))
-
-    @pl.loop(1, 8)
-    def _(delta):
-        greet(device((y + delta) % 8, zh, x, zl, core))
 
     quarter = zl * 2 + core
     own_tok = pltpu.make_async_copy(tok_in, tok.at[z, core], tok_sem.at[0])
@@ -124,7 +118,7 @@
     for copy in [own_tok, own_w, own_filt] + own_params + own_tables:
         copy.start()
 
-    pl.semaphore_wait(barrier, 25)
+    pl.semaphore_wait(barrier, 10)
 
     def remote(src, dst, send, recv, target):
         return pltpu.make_async_remote_copy(
@@ -210,18 +204,6 @@
         return remote(
             pstage, pbuf, p_send.at[delta], p_recv.at[0], device(y, zh, x, mate // 2, mate % 2)
         )
-
-    for i in range(8):
-        @pl.when(jnp.logical_not(at_home & (own_block == i)))
-        def _():
-            f_step(i).start()
-
-    @pl.when(at_home)
-    def _():
-        pltpu.make_async_copy(
-            fstage.at[pl.ds(pl.multiple_of(own_block * 16, 16), 16)], fmid.at[zl, zh],
-            f_recv.at[0],
-        ).start()
 
     @pl.when(mirrored)
     def _():
@@ -365,19 +347,6 @@
     pass_weights(2, 2)
     pass_weights(2, 3)
 
-    pltpu.make_async_copy(fmid, fmid, f_recv.at[0]).wait()
-    for side in range(2):
-        for from_zh in range(4):
-            piece = fmid[side, from_zh].astype(F32)
-            for j in range(2):
-                fwide[pl.ds(side * 128 + from_zh * 2 + j, 16, stride=8), :] = piece[
-                    :, j * 128 : (j + 1) * 128
-                ]
-    fturn[...] = fwide[...].astype(BF16).reshape(8, 32, 128)
-    for delta in range(1, 8):
-        g_step(delta).start()
-    pltpu.make_async_copy(fturn.at[y], fbuf.at[y], g_recv.at[0]).start()
-
     await_sibling(2)
     pass_weights(3, 0)
     pass_tokens(3, 0)
@@ -392,6 +361,43 @@
     project(0, [3])
     project(1, [3])
 
+    for k in range(4):
+        pass_weights(4, k)
+    project(0, [4])
+    project(1, [4])
+    project(2, [4])
+    pass_tokens(4, 0)
+    await_sibling(4)
+    for i in range(8):
+        @pl.when(jnp.logical_not(at_home & (own_block == i)))
+        def _():
+            f_step(i).start()
+
+    @pl.when(at_home)
+    def _():
+        pltpu.make_async_copy(
+            fstage.at[pl.ds(pl.multiple_of(own_block * 16, 16), 16)], fmid.at[zl, zh],
+            f_recv.at[0],
+        ).start()
+
+    project(3, [0, 1, 2, 3, 4])
+    reduce_early()
+
+    pltpu.make_async_copy(fmid, fmid, f_recv.at[0]).wait()
+    for side in range(2):
+        for from_zh in range(4):
+            piece = fmid[side, from_zh].astype(F32)
+            for j in range(2):
+                fwide[pl.ds(side * 128 + from_zh * 2 + j, 16, stride=8), :] = piece[
+                    :, j * 128 : (j + 1) * 128
+                ]
+    fturn[...] = fwide[...].astype(BF16).reshape(8, 32, 128)
+    for delta in range(1, 8):
+        g_step(delta).start()
+    pltpu.make_async_copy(fturn.at[y], fbuf.at[y], g_recv.at[0]).start()
+
+    reduce_late()
+
     pltpu.make_async_copy(fbuf, fbuf, g_recv.at[0]).wait()
     pltpu.make_async_copy(pbuf, pbuf, p_recv.at[0]).wait()
     for copy in own_tables:
@@ -405,17 +411,6 @@
             )
         )
     spectrum[...] = transform(jnp.concatenate(lanes, 1)) * (1.0 / 8192.0)
-
-    for k in range(4):
-        pass_weights(4, k)
-    project(0, [4])
-    project(1, [4])
-    project(2, [4])
-    pass_tokens(4, 0)
-    await_sibling(4)
-    project(3, [0, 1, 2, 3, 4])
-    reduce_early()
-    reduce_late()
 
     channel = 64 * (zh % 2) + 32 * zl + 16 * core + 4 * (y % 4)
     lane_at = lax.broadcasted_iota(jnp.int32, (16, 128), 1)

time: 71.1 us -> 68.7 us (0.966)
  Pallas kernels: 69.5 us -> 67.1 us
    pallas_call x1, Pallas kernels: 69.5 us -> 67.1 us  [per_device(): pl.pallas_call(kernel, out_shape=jax.ShapeDtypeStruct((128, 256), BF16),...]
where the time goes in v3:
time: 68.7 us; the launch traced here: 68.6 us
  Pallas kernels  67.1 us (98%)
  local copies, waits for them, and re-layouts  1.47 us (2%)
    pallas_call x1, Pallas kernels, per_device(): pl.pallas_call(kernel, out_shape=jax.ShapeDtypeStruct((128, 256), BF16),...  67.1 us
    unnamed x1, local copies, waits for them, and re-layouts  1.47 us

profile of v3, /device:TPU:1, one launch (start us, length us, event | category | flops | bytes accessed | tf_op | source)
XLA Modules:
  0.0 68.6 jit_solution(2664826455559686751)
XLA Ops:
  0.0 67.1 %shard_map.91 = bf16[128,256]{1,0:T(8,128)(2,1)} custom-call(bf16[2,128,512]{2,1,0:T(8,128)(2,1)} %bitcast.5, bf16[3,4,16,512]{3,2,1,0:T(8,128)(2,1)} %bitcast.6, f32[3,3,128]{2,1,0:T(4,128)} %short_in.1, f32[128,256]{1,0:T(8,128)} %filt_in.1, f32[1,128]{1,0:T(1,128)} %bitcast.7, f32[128,64]{1,0:T(8,128)} %constant.8.clone.first_in, ...), custom_call_target="tpu_custom_call" | custom-call | tf_op jit(solution)/shard_map/pallas_call | solution.py:554
  67.1 1.5 %copy.11 = bf16[128,256]{1,0:T(8,128)(2,1)} copy(bf16[128,256]{1,0:T(8,128)(2,1)} %shard_map.91) | data formatting | bytes 131072

commit v4 on v3

--- a/solution.py
+++ b/solution.py
@@ -8,6 +8,7 @@
 
 MESH = pl.DeviceIdType.MESH
 F32 = jnp.float32
+FAR_FIRST = (4, 3, 5, 2, 6, 1, 7)
 BF16 = jnp.bfloat16
 
 
@@ -60,6 +61,7 @@
     fstage, fmid, fwide, fturn, fbuf, pstage, pbuf, spectrum, oturn, omid, ostage,
     in_sem, tok_sem, own_sem, param_sem, table_sem,
     tok_send, tok_recv, sib_send, sib_recv, wa_send, wa_recv, wr_send, wr_recv,
+    ws_send, ws_recv,
     x_send, x_recv, e_send, e_recv, a_send, a_recv, f_send, f_recv, g_send, g_recv, p_send, p_recv,
     n_send, n_recv, o_send, o_recv,
 ):
@@ -92,17 +94,25 @@
     def greet(target):
         pl.semaphore_signal(barrier, inc=1, device_id=target, device_id_type=MESH)
 
-    greet(device_z((z + 1) % 8))
-    greet(device_z((z + 7) % 8))
-    greet(device((y + 1) % 8, zh, x, zl, core))
-    greet(device((y + 7) % 8, zh, x, zl, core))
+    @pl.when(core == 0)
+    def _():
+        greet(device_z((z + 1) % 8))
+        greet(device_z((z + 7) % 8))
+
+    @pl.when(core == 1)
+    def _():
+        greet(device((y + 1) % 8, zh, x, zl, core))
+        greet(device((y + 7) % 8, zh, x, zl, core))
+
     for delta in range(1, 4):
         mate = (zl * 2 + core + delta) % 4
         greet(device(y, zh, x, mate // 2, mate % 2))
         greet(device(y, zh, (x + delta) % 4, zl, core))
 
     quarter = zl * 2 + core
-    own_tok = pltpu.make_async_copy(tok_in, tok.at[z, core], tok_sem.at[0])
+    own_tok = [
+        pltpu.make_async_copy(tok_in.at[c], tok.at[z, c, core], tok_sem.at[c]) for c in range(2)
+    ]
     own_w = pltpu.make_async_copy(w_in, wown, own_sem.at[0])
     own_filt = pltpu.make_async_copy(filt_in, filt, in_sem.at[0])
     own_params = [
@@ -115,10 +125,10 @@
         pltpu.make_async_copy(second_in, second, table_sem.at[2]),
         pltpu.make_async_copy(last_in, last, table_sem.at[3]),
     ]
-    for copy in [own_tok, own_w, own_filt] + own_params + own_tables:
+    for copy in own_tok + [own_w, own_filt] + own_params + own_tables:
         copy.start()
 
-    pl.semaphore_wait(barrier, 10)
+    pl.semaphore_wait(barrier, 8)
 
     def remote(src, dst, send, recv, target):
         return pltpu.make_async_remote_copy(
@@ -126,55 +136,107 @@
             device_id=target, device_id_type=MESH,
         )
 
-    def tok_step(way, d, c):
+    def ends(way, k):
+        return k // 2 ^ way, k % 2
+
+    def goes(d, way, k):
+        return d < 4 or k < 2
+
+    def w_goes(d, way, k):
+        return d < 4 or k == way
+
+    def tok_step(way, d, k):
         shard = (z - (d - 1)) % 8 if way == 0 else (z + (d - 1)) % 8
         target = device_z((z + 1) % 8 if way == 0 else (z + 7) % 8)
-        ref = tok.at[shard, core, c]
-        return remote(
-            ref, ref, tok_send.at[way, d - 1, c], tok_recv.at[way, d - 1, c], target
-        )
-
-    def sib_step(slot, c):
-        ref = tok.at[(z - slot) % 8, core, c]
+        part, side = ends(way, k)
+        ref = tok.at[shard, part, side]
+        return remote(
+            ref, ref, tok_send.at[way, d - 1, k], tok_recv.at[way, d - 1, k], target
+        )
+
+    def swap_step(part):
+        ref = tok.at[z, part, core]
+        return remote(ref, ref, sib_send.at[0, part], sib_recv.at[0, part], sibling)
+
+    def sib_step(way, d, k):
+        slot = sib_slot(way, d)
+        part, side = ends(way, k)
+        ref = tok.at[(z - slot) % 8, part, side]
+        c = part * 2 + side
         return remote(ref, ref, sib_send.at[slot, c], sib_recv.at[slot, c], sibling)
+
+    def sib_slot(way, d):
+        return d if way == 0 else 8 - d
+
+    def half_of(k):
+        return zl if k == 0 else 1 - zl
 
     def w_step(way, d, k):
         shard = (y - (d - 1)) % 8 if way == 0 else (y + (d - 1)) % 8
         target = device((y + 1) % 8 if way == 0 else (y + 7) % 8, zh, x, zl, core)
-        ref = wbuf.at[shard, held(k)]
+        ref = wbuf.at[shard, half_of(k)]
         return remote(
             ref, ref, wr_send.at[way, d - 1, k], wr_recv.at[way, d - 1, k], target
         )
 
-    def held(k):
-        flipped = core if k % 2 == 0 else 1 - core
-        return (zl if k < 2 else 1 - zl) * 2 + flipped
-
-    def goes(d, way, k):
-        return d < 4 or k < 1
-
-    def wa_step(k):
-        mate = held(k)
-        return remote(
-            wown.at[:, mate], wbuf.at[y, quarter], wa_send.at[k], wa_recv.at[k],
-            device(y, zh, x, mate // 2, mate % 2),
-        )
-
-    def ends(way, k):
-        return k if way == 0 else 1 - k
+    def ws_step(slot, k):
+        ref = wbuf.at[(y - slot) % 8, half_of(k), 0]
+        return remote(ref, ref, ws_send.at[slot, k], ws_recv.at[slot, k], sibling)
+
+    def wa_step(k, owner):
+        source = wown.at[:, half_of(k) * 2 + owner]
+        landing = wbuf.at[y, zl, owner, core]
+        slot = k * 2 + core
+        return remote(
+            source, landing, wa_send.at[k, owner], wa_recv.at[slot, owner],
+            device(y, zh, x, half_of(k), 1),
+        )
+
+    def wa_arrival(k, side, owner):
+        landing = wbuf.at[y, half_of(k), owner, side]
+        return remote(
+            landing, landing, wa_send.at[k, owner], wa_recv.at[k * 2 + side, owner], sibling
+        )
+
+    for copy in own_tok:
+        copy.wait()
+    for part in range(2):
+        swap_step(part).start()
+
+    @pl.when(core == 0)
+    def _():
+        for way in range(2):
+            tok_step(way, 1, 0).start()
 
     own_w.wait()
-    for k in range(1, 4):
-        wa_step(k).start()
-    wbuf[y, quarter] = wown[:, quarter]
-    own_tok.wait()
-    for k in range(2):
+    for owner in range(2):
+        wa_step(1, owner).start()
+
+    @pl.when(core == 0)
+    def _():
+        for owner in range(2):
+            wa_step(0, owner).start()
+
+    @pl.when(core == 1)
+    def _():
+        for owner in range(2):
+            wbuf[y, zl, owner, 1] = wown[:, zl * 2 + owner]
+
+    @pl.when(core == 0)
+    def _():
+        for part in range(2):
+            swap_step(part).wait_recv()
+        for k in range(1, 4):
+            for way in range(2):
+                tok_step(way, 1, k).start()
+
+    @pl.when(core == 1)
+    def _():
+        for owner in range(2):
+            wa_arrival(0, 0, owner).wait_recv()
         for way in range(2):
-            if k == 0:
-                w_step(way, 1, 0).start()
-            tok_step(way, 1, ends(way, k)).start()
-    for c in range(2):
-        sib_step(0, c).start()
+            w_step(way, 1, 0).start()
+        ws_step(0, 0).start()
 
     own_filt.wait()
     fstage[...] = filt[...].astype(BF16)
@@ -211,31 +273,58 @@
         for delta in range(1, 4):
             p_step(delta).start()
 
-    for k in range(1, 4):
-        wa_step(k).wait_recv()
-        for way in range(2):
-            w_step(way, 1, k).start()
-
     def pass_tokens(d, k):
         for way in range(2):
-            c = ends(way, k)
-            tok_step(way, d, c).wait_recv()
+            tok_step(way, d, k).wait_recv()
             if d < 4 and goes(d + 1, way, k):
-                tok_step(way, d + 1, c).start()
-            sib_step(d if way == 0 else 8 - d, c).start()
+                tok_step(way, d + 1, k).start()
+            sib_step(way, d, k).start()
 
     def pass_weights(d, k):
         for way in range(2):
-            if d < 4 or k // 2 == way:
+            if w_goes(d, way, k):
                 w_step(way, d, k).wait_recv()
-                if d < 3 or (d == 3 and k // 2 == way):
+                if d < 4 and w_goes(d + 1, way, k):
                     w_step(way, d + 1, k).start()
-
-    def await_sibling(d):
-        for half in range(2):
-            for way in range(2):
-                if (0 < d < 4) or (d == 0 and way == 0) or (d == 4 and half == way):
-                    sib_step(0 if d == 0 else (d if way == 0 else 8 - d), half).wait_recv()
+                ws_step(sib_slot(way, d), k).start()
+
+    def await_tokens(d):
+        @pl.when(core == 1)
+        def _():
+            if d == 0:
+                for part in range(2):
+                    swap_step(part).wait_recv()
+            else:
+                for k in range(4):
+                    for way in range(2):
+                        if goes(d, way, k):
+                            sib_step(way, d, k).wait_recv()
+
+    def await_weights(d):
+        @pl.when(core == 0)
+        def _():
+            for k in range(2):
+                for way in range(2):
+                    if w_goes(d, way, k) and (d > 0 or way == 0):
+                        ws_step(sib_slot(way, d) % 8, k).wait_recv()
+
+    @pl.when(core == 0)
+    def _():
+        for d in range(1, 3):
+            for k in range(4):
+                pass_tokens(d, k)
+
+    @pl.when(core == 1)
+    def _():
+        for side in range(2):
+            for owner in range(2):
+                wa_arrival(1, side, owner).wait_recv()
+        for way in range(2):
+            w_step(way, 1, 1).start()
+        ws_step(0, 1).start()
+        for d in range(1, 4):
+            for k in range(2):
+                pass_weights(d, k)
 
     sign = 2 * zl - 1
     blocks = [zh, (zh + sign) % 4, (zh - sign) % 4, (zh + 2) % 4]
@@ -252,8 +341,10 @@
         total = jnp.zeros((48 * len(rows), 256), F32)
         for half in range(2):
             for side in range(2):
-                left = jnp.concatenate([wbuf[row, half * 2 + side].reshape(48, 512) for row in rows], 0)
-                right = tok[blocks[p] * 2 + half, side].reshape(256, 512)
+                left = jnp.concatenate(
+                    [wbuf[row, half, core, side].reshape(48, 512) for row in rows], 0
+                )
+                right = tok[blocks[p] * 2 + half, :, side].reshape(256, 512)
                 total = total + lax.dot_general(
                     left, right, (((1,), (1,)), ((), ())), preferred_element_type=F32
                 )
@@ -298,25 +389,21 @@
             device(target, zh, x, zl, core),
         )
 
-    padding = jnp.zeros((8, 128), F32)
-
-    def reduce_early():
-        for p in range(3):
+    def reduce_pair(first_block, packed, step, landed, arrived):
+        for p in (first_block, first_block + 1):
             sum_over_x(p)
         for target in range(8):
-            parts = pieces(0, target) + pieces(1, target) + pieces(2, target)
-            aearly[target] = jnp.concatenate(parts + [padding], 0).astype(BF16)
-        for delta in range(1, 8):
-            e_step(delta).start()
-        pltpu.make_async_copy(aearly.at[y], xearly.at[y], e_recv.at[0]).start()
+            parts = pieces(first_block, target) + pieces(first_block + 1, target)
+            packed[target] = jnp.concatenate(parts, 0).astype(BF16)
+        for delta in FAR_FIRST:
+            step(delta).start()
+        pltpu.make_async_copy(packed.at[y], landed.at[y], arrived.at[0]).start()
+
+    def reduce_early():
+        reduce_pair(0, aearly, e_step, xearly, e_recv)
 
     def reduce_late():
-        sum_over_x(3)
-        for target in range(8):
-            alate[target] = jnp.concatenate(pieces(3, target) + [padding], 0).astype(BF16)
-        for delta in range(1, 8):
-            a_step(delta).start()
-        pltpu.make_async_copy(alate.at[y], xlate.at[y], a_recv.at[0]).start()
+        reduce_pair(2, alate, a_step, xlate, a_recv)
 
     def transform(value):
         stage = table_left(first[...], value)
@@ -331,43 +418,36 @@
             )
         return table_right(jnp.concatenate(rows, 0), second[...])
 
-    pass_weights(1, 0)
-    pass_tokens(1, 0)
-    pass_weights(1, 1)
-    pass_tokens(1, 1)
-    pass_weights(1, 2)
-    pass_weights(1, 3)
-    await_sibling(0)
-    await_sibling(1)
-    pass_weights(2, 0)
-    pass_tokens(2, 0)
-    pass_weights(2, 1)
-    project(0, [0, 1])
-    pass_tokens(2, 1)
-    pass_weights(2, 2)
-    pass_weights(2, 3)
-
-    await_sibling(2)
-    pass_weights(3, 0)
-    pass_tokens(3, 0)
-    pass_weights(3, 1)
-    project(0, [2])
-    project(1, [0, 1, 2])
-    pass_tokens(3, 1)
-    pass_weights(3, 2)
-    pass_weights(3, 3)
-    await_sibling(3)
-    project(2, [0, 1, 2, 3])
-    project(0, [3])
-    project(1, [3])
-
-    for k in range(4):
-        pass_weights(4, k)
+    @pl.when(core == 0)
+    def _():
+        for k in range(4):
+            pass_tokens(3, k)
+
+    await_tokens(0)
+    await_tokens(1)
+    for d in range(4):
+        await_weights(d)
+    project(0, [0, 1, 2, 3])
+    await_tokens(2)
+    project(1, [0, 1, 2, 3])
+
+    @pl.when(core == 1)
+    def _():
+        for k in range(2):
+            pass_weights(4, k)
+
+    await_weights(4)
     project(0, [4])
     project(1, [4])
-    project(2, [4])
-    pass_tokens(4, 0)
-    await_sibling(4)
+    await_tokens(3)
+    project(2, [0, 1, 2, 3, 4])
+
+    @pl.when(core == 0)
+    def _():
+        for k in range(2):
+            pass_tokens(4, k)
+
+    await_tokens(4)
     for i in range(8):
         @pl.when(jnp.logical_not(at_home & (own_block == i)))
         def _():
@@ -392,11 +472,42 @@
                     :, j * 128 : (j + 1) * 128
                 ]
     fturn[...] = fwide[...].astype(BF16).reshape(8, 32, 128)
-    for delta in range(1, 8):
+    for delta in FAR_FIRST:
         g_step(delta).start()
     pltpu.make_async_copy(fturn.at[y], fbuf.at[y], g_recv.at[0]).start()
 
     reduce_late()
+
+    @pl.when(core == 0)
+    def _():
+        for owner in range(2):
+            wa_step(0, owner).wait_send()
+        for d in range(1, 5):
+            for k in range(4):
+                for way in range(2):
+                    if goes(d, way, k):
+                        tok_step(way, d, k).wait_send()
+                        sib_step(way, d, k).wait_send()
+
+    @pl.when(core == 1)
+    def _():
+        for k in range(2):
+            ws_step(0, k).wait_send()
+        for d in range(1, 5):
+            for k in range(2):
+                for way in range(2):
+                    if w_goes(d, way, k):
+                        w_step(way, d, k).wait_send()
+                        ws_step(sib_slot(way, d), k).wait_send()
+
+    for owner in range(2):
+        wa_step(1, owner).wait_send()
+        swap_step(owner).wait_send()
+    for p in range(4):
+        for row in range(8):
+            @pl.when(row // 2 != x)
+            def _():
+                x_step(p, row).wait_send()
 
     pltpu.make_async_copy(fbuf, fbuf, g_recv.at[0]).wait()
     pltpu.make_async_copy(pbuf, pbuf, p_recv.at[0]).wait()
@@ -412,6 +523,20 @@
         )
     spectrum[...] = transform(jnp.concatenate(lanes, 1)) * (1.0 / 8192.0)
 
+    for delta in FAR_FIRST:
+        e_step(delta).wait_send()
+        g_step(delta).wait_send()
+
+    @pl.when(mirrored)
+    def _():
+        for delta in range(1, 4):
+            p_step(delta).wait_send()
+
+    for i in range(8):
+        @pl.when(jnp.logical_not(at_home & (own_block == i)))
+        def _():
+            f_step(i).wait_send()
+
     channel = 64 * (zh % 2) + 32 * zl + 16 * core + 4 * (y % 4)
     lane_at = lax.broadcasted_iota(jnp.int32, (16, 128), 1)
     gains = [
@@ -419,11 +544,13 @@
         for ch in range(4)
     ]
     pltpu.make_async_copy(xearly, xearly, e_recv.at[0]).wait()
-    early = xearly[...].astype(F32)
-    for p in range(3):
-        xwide[blocks[p]] = early[:, p * 24 : (p + 1) * 24, :].reshape(192, 128)
+    wide = xearly[...].astype(F32)
+    for p in range(2):
+        xwide[blocks[p]] = wide[:, p * 24 : (p + 1) * 24, :].reshape(192, 128)
     pltpu.make_async_copy(xlate, xlate, a_recv.at[0]).wait()
-    xwide[blocks[3]] = xlate[...].astype(F32)[:, :24, :].reshape(192, 128)
+    wide = xlate[...].astype(F32)
+    for p in range(2):
+        xwide[blocks[2 + p]] = wide[:, p * 24 : (p + 1) * 24, :].reshape(192, 128)
     lane = lax.broadcasted_iota(jnp.int32, (64, 128), 1)
     below = lax.broadcasted_iota(jnp.int32, (8, 128), 0)
 
@@ -481,7 +608,7 @@
             device(target, zh, x, zl, core),
         )
 
-    for delta in range(1, 8):
+    for delta in FAR_FIRST:
         n_step(delta).start()
     pltpu.make_async_copy(oturn.at[y], omid.at[y], n_recv.at[0]).start()
 
@@ -506,41 +633,12 @@
     def _():
         pltpu.make_async_copy(ostage.at[own_out], out_rows, o_recv.at[0]).start()
 
-    for d in range(1, 5):
-        for k in range(4):
-            for way in range(2):
-                if k < 2 and goes(d, way, k):
-                    tok_step(way, d, ends(way, k)).wait_send()
-                if d < 4 or k // 2 == way:
-                    w_step(way, d, k).wait_send()
-    for slot in range(8):
-        for half in range(2):
-            sib_step(slot, half).wait_send()
-    for k in range(1, 4):
-        wa_step(k).wait_send()
-    for p in range(4):
-        for row in range(8):
-            @pl.when(row // 2 != x)
-            def _():
-                x_step(p, row).wait_send()
-
-    @pl.when(mirrored)
-    def _():
-        for delta in range(1, 4):
-            p_step(delta).wait_send()
-
     for i in range(8):
-        @pl.when(jnp.logical_not(at_home & (own_block == i)))
-        def _():
-            f_step(i).wait_send()
-
         @pl.when(jnp.logical_not(at_home & (own_out == i)))
         def _():
             o_step(i).wait_send()
 
-    for delta in range(1, 8):
-        g_step(delta).wait_send()
-        e_step(delta).wait_send()
+    for delta in FAR_FIRST:
         a_step(delta).wait_send()
         n_step(delta).wait_send()
     pltpu.make_async_copy(out, out, o_recv.at[0]).wait()
@@ -566,14 +664,14 @@
             pltpu.VMEM((128, 256), F32),
             pltpu.VMEM((8, 2, 2, 128, 512), BF16),
             pltpu.VMEM((3, 4, 16, 512), BF16),
-            pltpu.VMEM((8, 4, 3, 16, 512), BF16),
+            pltpu.VMEM((8, 2, 2, 2, 3, 16, 512), BF16),
             pltpu.VMEM((4, 8, 48, 256), BF16),
             pltpu.VMEM((4, 4, 2, 48, 256), BF16),
             pltpu.VMEM((4, 192, 128), F32),
-            pltpu.VMEM((8, 80, 128), BF16),
-            pltpu.VMEM((8, 80, 128), BF16),
-            pltpu.VMEM((8, 32, 128), BF16),
-            pltpu.VMEM((8, 32, 128), BF16),
+            pltpu.VMEM((8, 48, 128), BF16),
+            pltpu.VMEM((8, 48, 128), BF16),
+            pltpu.VMEM((8, 48, 128), BF16),
+            pltpu.VMEM((8, 48, 128), BF16),
             pltpu.VMEM((4, 192, 128), F32),
             pltpu.VMEM((128, 256), BF16),
             pltpu.VMEM((2, 4, 16, 256), BF16),
@@ -586,11 +684,12 @@
             pltpu.VMEM((8, 32, 128), BF16),
             pltpu.VMEM((8, 32, 128), BF16),
             pltpu.VMEM((8, 16, 256), BF16),
-            dma((1,)), dma((1,)), dma((1,)), dma((2,)), dma((4,)),
+            dma((1,)), dma((2,)), dma((1,)), dma((2,)), dma((4,)),
+            dma((2, 4, 4)), dma((2, 4, 4)),
+            dma((8, 4)), dma((8, 4)),
+            dma((2, 2)), dma((4, 2)),
             dma((2, 4, 2)), dma((2, 4, 2)),
             dma((8, 2)), dma((8, 2)),
-            dma((4,)), dma((4,)),
-            dma((2, 4, 4)), dma((2, 4, 4)),
             dma((4, 8)), dma((4,)),
             dma((8,)), dma((1,)),
             dma((8,)), dma((1,)),

time: 68.7 us -> 66.7 us (0.971)
  Pallas kernels: 67.1 us -> 65.1 us
    pallas_call x1, Pallas kernels: 67.1 us -> 65.1 us  [per_device(): pl.pallas_call(kernel, out_shape=jax.ShapeDtypeStruct((128, 256), BF16),...]
where the time goes in v4:
time: 66.7 us; the launch traced here: 66.5 us
  Pallas kernels  65.1 us (98%)
  local copies, waits for them, and re-layouts  1.47 us (2%)
    pallas_call x1, Pallas kernels, per_device(): pl.pallas_call(kernel, out_shape=jax.ShapeDtypeStruct((128, 256), BF16),...  65.1 us
    unnamed x1, local copies, waits for them, and re-layouts  1.47 us

profile of v4, /device:TPU:1, one launch (start us, length us, event | category | flops | bytes accessed | tf_op | source)
XLA Modules:
  0.0 66.5 jit_solution(10725248696381517718)
XLA Ops:
  0.0 65.1 %shard_map.91 = bf16[128,256]{1,0:T(8,128)(2,1)} custom-call(bf16[2,128,512]{2,1,0:T(8,128)(2,1)} %bitcast.5, bf16[3,4,16,512]{3,2,1,0:T(8,128)(2,1)} %bitcast.6, f32[3,3,128]{2,1,0:T(4,128)} %short_in.1, f32[128,256]{1,0:T(8,128)} %filt_in.1, f32[1,128]{1,0:T(1,128)} %bitcast.7, f32[128,64]{1,0:T(8,128)} %constant.8.clone.first_in, ...), custom_call_target="tpu_custom_call" | custom-call | tf_op jit(solution)/shard_map/pallas_call | solution.py:652
  65.1 1.5 %copy.11 = bf16[128,256]{1,0:T(8,128)(2,1)} copy(bf16[128,256]{1,0:T(8,128)(2,1)} %shard_map.91) | data formatting | bytes 131072

commit v5 on v4

--- a/solution.py
+++ b/solution.py
@@ -58,7 +58,7 @@
     out,
     first, twist, second, last, short, skip, filt,
     tok, wown, wbuf, sbuf, rbuf, sums, aearly, xearly, alate, xlate, xwide,
-    fstage, fmid, fwide, fturn, fbuf, pstage, pbuf, spectrum, oturn, omid, ostage,
+    fstage, fmid, fwide, fturn, fbuf, pstage, pbuf, spectrum, owide, oturn, omid, ostage,
     in_sem, tok_sem, own_sem, param_sem, table_sem,
     tok_send, tok_recv, sib_send, sib_recv, wa_send, wa_recv, wr_send, wr_recv,
     ws_send, ws_recv,
@@ -87,6 +87,7 @@
 
     at_home = core == zh // 2
     own_block = (zh % 2) * 4 + zl * 2 + core
+    between = zl == y // 4
     own_out = zl * 4 + zh
 
     barrier = pltpu.get_barrier_semaphore()
@@ -114,7 +115,10 @@
         pltpu.make_async_copy(tok_in.at[c], tok.at[z, c, core], tok_sem.at[c]) for c in range(2)
     ]
     own_w = pltpu.make_async_copy(w_in, wown, own_sem.at[0])
-    own_filt = pltpu.make_async_copy(filt_in, filt, in_sem.at[0])
+    own_filt = [
+        pltpu.make_async_copy(filt_in.at[:, pl.ds(j * 128, 128)], filt.at[j], in_sem.at[j])
+        for j in range(2)
+    ]
     own_params = [
         pltpu.make_async_copy(short_in, short, param_sem.at[0]),
         pltpu.make_async_copy(skip_in, skip, param_sem.at[1]),
@@ -125,7 +129,7 @@
         pltpu.make_async_copy(second_in, second, table_sem.at[2]),
         pltpu.make_async_copy(last_in, last, table_sem.at[3]),
     ]
-    for copy in own_tok + [own_w, own_filt] + own_params + own_tables:
+    for copy in own_tok + [own_w] + own_filt + own_params + own_tables:
         copy.start()
 
     pl.semaphore_wait(barrier, 8)
@@ -238,8 +242,15 @@
             w_step(way, 1, 0).start()
         ws_step(0, 0).start()
 
-    own_filt.wait()
-    fstage[...] = filt[...].astype(BF16)
+    for copy in own_filt:
+        copy.wait()
+    for k in range(4):
+        tiles = [
+            filt[j, pl.ds(k * 4 + ch, 8, stride=16), :]
+            for ch in range(4)
+            for j in range(2)
+        ]
+        fstage[k] = jnp.concatenate(tiles, 0).astype(BF16)
     for copy in own_params:
         copy.wait()
     pstage[...] = jnp.zeros_like(pstage)
@@ -248,17 +259,15 @@
             pstage[i * 3 + b : i * 3 + b + 1, :] = short[i, b : b + 1, :]
     pstage[9:10, :] = skip[...]
 
-    def f_step(i):
-        return remote(
-            fstage.at[pl.ds(i * 16, 16)], fmid.at[zl, zh], f_send.at[i], f_recv.at[0],
-            filter_holder(i),
-        )
-
-    def g_step(delta):
-        target = (y + delta) % 8
-        return remote(
-            fturn.at[target], fbuf.at[y], g_send.at[delta], g_recv.at[0],
-            device(target, zh, x, zl, core),
+    def f_step(k):
+        return remote(
+            fstage.at[k], fmid.at[y], f_send.at[k], f_recv.at[0],
+            device(4 * zl + k, zh, x, zl, core),
+        )
+
+    def g_step(i):
+        return remote(
+            fturn.at[i], fbuf.at[zh], g_send.at[i], g_recv.at[0], filter_holder(i)
         )
 
     def p_step(delta):
@@ -437,6 +446,15 @@
             pass_weights(4, k)
 
     await_weights(4)
+    for k in range(4):
+        @pl.when(4 * zl + k != y)
+        def _():
+            f_step(k).start()
+
+    @pl.when(between)
+    def _():
+        pltpu.make_async_copy(fstage.at[y % 4], fmid.at[y], f_recv.at[0]).start()
+
     project(0, [4])
     project(1, [4])
     await_tokens(3)
@@ -448,33 +466,24 @@
             pass_tokens(4, k)
 
     await_tokens(4)
-    for i in range(8):
-        @pl.when(jnp.logical_not(at_home & (own_block == i)))
+    project(3, [0, 1, 2, 3, 4])
+    @pl.when(between)
+    def _():
+        pltpu.make_async_copy(fmid, fmid, f_recv.at[0]).wait()
+        fwide[...] = fmid[...].astype(F32).reshape(512, 128)
+        for i in range(8):
+            tiles = [fwide[pl.ds(n * 8 + i, 8, stride=64), :] for n in range(8)]
+            fturn[i] = jnp.concatenate(tiles, 0).astype(BF16)
+        for i in range(8):
+            @pl.when(jnp.logical_not(at_home & (own_block == i)))
+            def _():
+                g_step(i).start()
+
+        @pl.when(at_home)
         def _():
-            f_step(i).start()
-
-    @pl.when(at_home)
-    def _():
-        pltpu.make_async_copy(
-            fstage.at[pl.ds(pl.multiple_of(own_block * 16, 16), 16)], fmid.at[zl, zh],
-            f_recv.at[0],
-        ).start()
-
-    project(3, [0, 1, 2, 3, 4])
+            pltpu.make_async_copy(fturn.at[own_block], fbuf.at[zh], g_recv.at[0]).start()
+
     reduce_early()
-
-    pltpu.make_async_copy(fmid, fmid, f_recv.at[0]).wait()
-    for side in range(2):
-        for from_zh in range(4):
-            piece = fmid[side, from_zh].astype(F32)
-            for j in range(2):
-                fwide[pl.ds(side * 128 + from_zh * 2 + j, 16, stride=8), :] = piece[
-                    :, j * 128 : (j + 1) * 128
-                ]
-    fturn[...] = fwide[...].astype(BF16).reshape(8, 32, 128)
-    for delta in FAR_FIRST:
-        g_step(delta).start()
-    pltpu.make_async_copy(fturn.at[y], fbuf.at[y], g_recv.at[0]).start()
 
     reduce_late()
 
@@ -513,29 +522,34 @@
     pltpu.make_async_copy(pbuf, pbuf, p_recv.at[0]).wait()
     for copy in own_tables:
         copy.wait()
-    fwide[...] = fbuf[...].astype(F32).reshape(256, 128)
+    wide = fbuf[...].astype(F32)
     lanes = []
     for ch in range(4):
         lanes.append(
             jnp.concatenate(
-                [fwide[pl.ds(ch * 8 + inner, 8, stride=32), :] for inner in range(8)], 0
+                [wide[n, (ch * 2 + j) * 8 : (ch * 2 + j + 1) * 8, :] for n in range(4) for j in range(2)],
+                0,
             )
         )
     spectrum[...] = transform(jnp.concatenate(lanes, 1)) * (1.0 / 8192.0)
 
     for delta in FAR_FIRST:
         e_step(delta).wait_send()
-        g_step(delta).wait_send()
 
     @pl.when(mirrored)
     def _():
         for delta in range(1, 4):
             p_step(delta).wait_send()
 
+    for k in range(4):
+        @pl.when(4 * zl + k != y)
+        def _():
+            f_step(k).wait_send()
+
     for i in range(8):
-        @pl.when(jnp.logical_not(at_home & (own_block == i)))
+        @pl.when(between & jnp.logical_not(at_home & (own_block == i)))
         def _():
-            f_step(i).wait_send()
+            g_step(i).wait_send()
 
     channel = 64 * (zh % 2) + 32 * zl + 16 * core + 4 * (y % 4)
     lane_at = lax.broadcasted_iota(jnp.int32, (16, 128), 1)
@@ -595,11 +609,11 @@
             convolved[:, ch * 128 : (ch + 1) * 128] + gains[ch][9:10, :] * drives[ch]
         )
         for inner in range(8):
-            fwide[pl.ds(ch * 8 + inner, 8, stride=32), :] = gated[
+            owide[pl.ds(ch * 8 + inner, 8, stride=32), :] = gated[
                 inner * 8 : (inner + 1) * 8, :
             ]
 
-    oturn[...] = fwide[...].astype(BF16).reshape(8, 32, 128)
+    oturn[...] = owide[...].astype(BF16).reshape(8, 32, 128)
 
     def n_step(delta):
         target = (y + delta) % 8
@@ -618,11 +632,11 @@
         return remote(ostage.at[i], out_rows, o_send.at[i], o_recv.at[0], out_owner(i))
 
     pltpu.make_async_copy(omid, omid, n_recv.at[0]).wait()
-    fwide[...] = omid[...].astype(F32).reshape(256, 128)
+    owide[...] = omid[...].astype(F32).reshape(256, 128)
     for i in range(8):
         first_row = (i // 4) * 128 + (i % 4) * 2
         ostage[i] = jnp.concatenate(
-            [fwide[pl.ds(first_row + j, 16, stride=8), :] for j in range(2)], 1
+            [owide[pl.ds(first_row + j, 16, stride=8), :] for j in range(2)], 1
         ).astype(BF16)
     for i in range(8):
         @pl.when(jnp.logical_not(at_home & (own_out == i)))
@@ -661,7 +675,7 @@
             pltpu.VMEM((64, 128), F32),
             pltpu.VMEM((3, 3, 128), F32),
             pltpu.VMEM((1, 128), F32),
-            pltpu.VMEM((128, 256), F32),
+            pltpu.VMEM((2, 128, 128), F32),
             pltpu.VMEM((8, 2, 2, 128, 512), BF16),
             pltpu.VMEM((3, 4, 16, 512), BF16),
             pltpu.VMEM((8, 2, 2, 2, 3, 16, 512), BF16),
@@ -673,18 +687,19 @@
             pltpu.VMEM((8, 48, 128), BF16),
             pltpu.VMEM((8, 48, 128), BF16),
             pltpu.VMEM((4, 192, 128), F32),
-            pltpu.VMEM((128, 256), BF16),
-            pltpu.VMEM((2, 4, 16, 256), BF16),
+            pltpu.VMEM((4, 64, 128), BF16),
+            pltpu.VMEM((8, 64, 128), BF16),
+            pltpu.VMEM((512, 128), F32),
+            pltpu.VMEM((8, 64, 128), BF16),
+            pltpu.VMEM((4, 64, 128), BF16),
+            pltpu.VMEM((16, 128), F32),
+            pltpu.VMEM((16, 128), F32),
+            pltpu.VMEM((256, 256), F32),
             pltpu.VMEM((256, 128), F32),
             pltpu.VMEM((8, 32, 128), BF16),
             pltpu.VMEM((8, 32, 128), BF16),
-            pltpu.VMEM((16, 128), F32),
-            pltpu.VMEM((16, 128), F32),
-            pltpu.VMEM((256, 256), F32),
-            pltpu.VMEM((8, 32, 128), BF16),
-            pltpu.VMEM((8, 32, 128), BF16),
             pltpu.VMEM((8, 16, 256), BF16),
-            dma((1,)), dma((2,)), dma((1,)), dma((2,)), dma((4,)),
+            dma((2,)), dma((2,)), dma((1,)), dma((2,)), dma((4,)),
             dma((2, 4, 4)), dma((2, 4, 4)),
             dma((8, 4)), dma((8, 4)),
             dma((2, 2)), dma((4, 2)),
@@ -693,7 +708,7 @@
             dma((4, 8)), dma((4,)),
             dma((8,)), dma((1,)),
             dma((8,)), dma((1,)),
-            dma((8,)), dma((1,)),
+            dma((4,)), dma((1,)),
             dma((8,)), dma((1,)),
             dma((4,)), dma((1,)),
             dma((8,)), dma((1,)),

time: 66.7 us -> 65 us (0.975)
  Pallas kernels: 65.1 us -> 63.3 us
    pallas_call x1, Pallas kernels: 65.1 us -> 63.3 us  [per_device(): pl.pallas_call(kernel, out_shape=jax.ShapeDtypeStruct((128, 256), BF16),...]
where the time goes in v5:
time: 65 us; the launch traced here: 64.8 us
  Pallas kernels  63.3 us (97%)
  local copies, waits for them, and re-layouts  1.47 us (2%)
    pallas_call x1, Pallas kernels, per_device(): pl.pallas_call(kernel, out_shape=jax.ShapeDtypeStruct((128, 256), BF16),...  63.3 us
    unnamed x1, local copies, waits for them, and re-layouts  1.47 us

profile of v5, /device:TPU:1, one launch (start us, length us, event | category | flops | bytes accessed | tf_op | source)
XLA Modules:
  0.0 64.8 jit_solution(9372764103642160929)
XLA Ops:
  0.0 63.3 %shard_map.91 = bf16[128,256]{1,0:T(8,128)(2,1)} custom-call(bf16[2,128,512]{2,1,0:T(8,128)(2,1)} %bitcast.5, bf16[3,4,16,512]{3,2,1,0:T(8,128)(2,1)} %bitcast.6, f32[3,3,128]{2,1,0:T(4,128)} %short_in.1, f32[128,256]{1,0:T(8,128)} %filt_in.1, f32[1,128]{1,0:T(1,128)} %bitcast.7, f32[128,64]{1,0:T(8,128)} %constant.8.clone.first_in, ...), custom_call_target="tpu_custom_call" | custom-call | tf_op jit(solution)/shard_map/pallas_call | solution.py:666
  63.3 1.5 %copy.11 = bf16[128,256]{1,0:T(8,128)(2,1)} copy(bf16[128,256]{1,0:T(8,128)(2,1)} %shard_map.91) | data formatting | bytes 131072

commit v6 on v5

--- a/solution.py
+++ b/solution.py
@@ -345,8 +345,12 @@
             device(y, zh, row // 2, zl, core),
         )
 
+    by_distance = [2 * ((x + hop) % 4) + part for hop in (2, 1, 3, 0) for part in range(2)]
+
     def project(p, steps):
         rows = [(y + delta) % 8 for step in steps for delta in near[step]]
+        if len(rows) == 8:
+            rows = by_distance
         total = jnp.zeros((48 * len(rows), 256), F32)
         for half in range(2):
             for side in range(2):

time: 65 us -> 65.1 us (level)
  no operation moved by 1% of the time
where the time goes in v6:
time: 65.1 us; the launch traced here: 64.9 us
  Pallas kernels  63.4 us (97%)
  local copies, waits for them, and re-layouts  1.47 us (2%)
    pallas_call x1, Pallas kernels, per_device(): pl.pallas_call(kernel, out_shape=jax.ShapeDtypeStruct((128, 256), BF16),...  63.4 us
    unnamed x1, local copies, waits for them, and re-layouts  1.47 us

profile of v6, /device:TPU:1, one launch (start us, length us, event | category | flops | bytes accessed | tf_op | source)
XLA Modules:
  0.0 64.9 jit_solution(17143570596957059614)
XLA Ops:
  0.0 63.4 %shard_map.91 = bf16[128,256]{1,0:T(8,128)(2,1)} custom-call(bf16[2,128,512]{2,1,0:T(8,128)(2,1)} %bitcast.5, bf16[3,4,16,512]{3,2,1,0:T(8,128)(2,1)} %bitcast.6, f32[3,3,128]{2,1,0:T(4,128)} %short_in.1, f32[128,256]{1,0:T(8,128)} %filt_in.1, f32[1,128]{1,0:T(1,128)} %bitcast.7, f32[128,64]{1,0:T(8,128)} %constant.8.clone.first_in, ...), custom_call_target="tpu_custom_call" | custom-call | tf_op jit(solution)/shard_map/pallas_call | solution.py:670
  63.4 1.5 %copy.11 = bf16[128,256]{1,0:T(8,128)(2,1)} copy(bf16[128,256]{1,0:T(8,128)(2,1)} %shard_map.91) | data formatting | bytes 131072
